TPU v7x, 32 devices: a whole 2x2x4 slice. The times are simulated.
32 devices in a mesh: cfg: 2 (over y), tm: 16 (over z, x, core).
Axes of the slice: x: 2, y: 2, z: 4, core: 2. Of those that a mesh axis runs over, the one named last changes fastest.
Arguments:
- meson_fields: bfloat16 [2, 32, 32, 256, 256], P(None, None, ('cfg', 'tm')), parts along dimension 2, may hold values from -1.3 to 1.3
- perambulators: bfloat16 [2, 32, 256, 256], P(None, ('cfg', 'tm')), parts along dimension 1, may hold values from -0.25 to 0.25
- direct_ins: int32 [4096, 4], replicated, may hold values from 0 to 31, as said below
- direct_coef: float32 [4096], replicated, may hold values from -5 to 5
- direct_entry: int32 [4096], replicated, may hold values from 0 to 63
- box_ins: int32 [8, 4], replicated, may hold values from 0 to 31, as said below
- box_coef: float32 [8], replicated, may hold values from -24 to 24
- box_entry: int32 [8], replicated, may hold values from 0 to 63
Outputs:
- correlator: float32 [3, 2, 128], P(None, None, ('cfg', 'tm')), parts along dimension 2
There are 2 independent parts, one for each index of `cfg`. A program takes and returns all parts, laid end to end along the dimension named above; an argument that names none is the same for every part. Nothing has to cross between parts.
Inputs may be any that keep to these rules, and one draw needn't show every extreme that they name: `direct_ins`: within a term, insertions 0 and 1 differ, 1 and 2 differ, 2 and 3 differ. `box_ins`: within a term, insertions 0 and 1 differ, 1 and 2 differ, 2 and 3 differ.
All inputs are finite; a program needn't handle non-finite values.
Results may differ from a plain program's by a relative error of at most 0.0046.
Values may be sent and summed in bfloat16 or wider, within the bound.
A program may use at most 192 MiB of HBM per device.

v0:
```python
import jax
import jax.numpy as jnp
from jax import lax
from jax.sharding import PartitionSpec as P

INSERTIONS = 32
ENTRY_DEV = 4


def from_behind(block, axis, distance):
    devices = range(lax.axis_size(axis))
    route = [((i - distance) % len(devices), i) for i in devices]
    return lax.ppermute(block, axis, route)


def one_hot(indices, length):
    return (indices[:, None] == jnp.arange(length, dtype=jnp.int32)[None, :]).astype(jnp.float32)


def lookup(table, left_hot, right_hot):
    picked = jnp.einsum("la,sab->slb", left_hot, table, precision=lax.Precision.HIGHEST)
    return jnp.sum(picked * right_hot[None], axis=2)


def adjoint_product(left_side, right_side):
    real_part = jnp.einsum(
        "slcij,slckj->slik", left_side, right_side, preferred_element_type=jnp.float32
    )
    imag_part = jnp.einsum(
        "slij,slkj->slik",
        left_side[:, :, 1],
        right_side[:, :, 0],
        preferred_element_type=jnp.float32,
    ) - jnp.einsum(
        "slij,slkj->slik",
        left_side[:, :, 0],
        right_side[:, :, 1],
        preferred_element_type=jnp.float32,
    )
    return (real_part, imag_part)


def pair_terms(sink_side, source, tables, entries):
    hots, direct_coef, direct_entry, box_ins, box_coef, box_entry = tables
    blocks, inserts = (sink_side.shape[0], sink_side.shape[1])
    sink_rows = sink_side.reshape(blocks, 2 * inserts, -1)
    source_rows = source.reshape(blocks, 2 * inserts, -1)
    correlations = jnp.einsum(
        "sam,sbm->sab", sink_rows, source_rows, preferred_element_type=jnp.float32
    )
    correlations = correlations.reshape(blocks, inserts, 2, inserts, 2)
    loop_real = correlations[:, :, 0, :, 0] + correlations[:, :, 1, :, 1]
    loop_imag = correlations[:, :, 1, :, 0] - correlations[:, :, 0, :, 1]
    real_left = lookup(loop_real, hots[0], hots[1])
    imag_left = lookup(loop_imag, hots[0], hots[1])
    real_right = lookup(loop_real, hots[2], hots[3])
    imag_right = lookup(loop_imag, hots[2], hots[3])
    direct_real = jnp.sum(direct_coef * (real_left * real_right - imag_left * imag_right), axis=0)
    direct_imag = jnp.sum(direct_coef * (real_left * imag_right + imag_left * real_right), axis=0)
    first_real, first_imag = adjoint_product(
        jnp.take(sink_side, box_ins[:, 0], axis=1), jnp.take(source, box_ins[:, 1], axis=1)
    )
    second_real, second_imag = adjoint_product(
        jnp.take(source, box_ins[:, 3], axis=1), jnp.take(sink_side, box_ins[:, 2], axis=1)
    )
    box_real = box_coef * jnp.sum(
        first_real * second_real + first_imag * second_imag, axis=(0, 2, 3)
    )
    box_imag = box_coef * jnp.sum(
        first_imag * second_real - first_real * second_imag, axis=(0, 2, 3)
    )
    direct_sum = jax.ops.segment_sum(
        jnp.stack([direct_real, direct_imag], 1), direct_entry, num_segments=entries
    )
    box_sum = jax.ops.segment_sum(
        jnp.stack([box_real, box_imag], 1), box_entry, num_segments=entries
    )
    return jnp.transpose(direct_sum - box_sum)


def local(
    meson_fields, perambulators, direct_ins, direct_coef, direct_entry, box_ins, box_coef, box_entry
):
    real_factor = jnp.stack([perambulators[0], -perambulators[1]], 0)
    imag_factor = jnp.stack([perambulators[1], perambulators[0]], 0)
    dressed_real = jnp.einsum(
        "cgsij,csjk->sgik", meson_fields, real_factor, preferred_element_type=jnp.float32
    )
    dressed_imag = jnp.einsum(
        "cgsij,csjk->sgik", meson_fields, imag_factor, preferred_element_type=jnp.float32
    )
    own_block = jnp.stack([dressed_real, dressed_imag], 2).astype(jnp.bfloat16)
    next_fields = from_behind(own_block, "tm", -1)
    far_fields = from_behind(next_fields, "tm", -1)
    entries = ENTRY_DEV * lax.axis_size("tm")
    hots = [one_hot(direct_ins[:, column], INSERTIONS) for column in range(4)]
    tables = (hots, direct_coef, direct_entry, box_ins, box_coef, box_entry)
    same_time = pair_terms(own_block, own_block, tables, entries)
    one_apart = pair_terms(own_block, next_fields, tables, entries)
    two_apart = pair_terms(own_block, far_fields, tables, entries)
    slices = own_block.shape[0] * lax.axis_size("tm")
    pieces = [
        lax.psum_scatter(partial_sum, "tm", scatter_dimension=1, tiled=True)
        for partial_sum in (same_time, one_apart, two_apart)
    ]
    summed = jnp.stack(pieces)
    return summed / slices


def solution(mesh):
    placed = (
        P(None, None, ("cfg", "tm"), None, None),
        P(None, ("cfg", "tm"), None, None),
        P(),
        P(),
        P(),
        P(),
        P(),
        P(),
    )
    return jax.shard_map(
        local, mesh=mesh, in_specs=placed, out_specs=P(None, None, ("cfg", "tm")), check_vma=False
    )
```

profile of v0, /device:TPU:0, one launch (start us, length us, event | category | flops | bytes accessed | tf_op | source)
XLA Modules:
  0.0 436.1 jit_solution(10730163838135135639)
XLA Ops:
  1.2 5.8 %bitcast_convert_fusion = bf16[256,32,256]{2,0,1:T(8,128)(2,1)S(1)} fusion(bf16[2,32,1,256,256]{4,3,2,1,0:T(8,128)(2,1)} %param.10, bf16[1,1,256,256]{2,3,0,1:T(8,128)(2,1)S(1)} %copy.356, bf16[1,1,256,256]{2,3,0,1:T(8,128)(2,1)S(1)} %copy.357), kind=kOutput, calls=%fused_computation.14 | convolution fusion | flops 2150105088 | bytes 12845056 | tf_op jit(solution)/shard_map/cgsij,csjk->sgik/dot_general | solution.py:89
  7.0 7.3 %bitcast_convert_fusion.1 = bf16[256,32,256]{2,0,1:T(8,128)(2,1)S(1)} fusion(bf16[2,32,1,256,256]{4,3,2,1,0:T(8,128)(2,1)} %param.10, bf16[1,1,256,256]{2,3,0,1:T(8,128)(2,1)S(1)} %neg.6, bf16[1,1,256,256]{2,3,0,1:T(8,128)(2,1)S(1)} %copy.356), kind=kOutput, calls=%fused_computation.15 | convolution fusion | flops 2150105088 | bytes 12845056 | tf_op jit(solution)/shard_map/cgsij,csjk->sgik/dot_general | solution.py:86
  14.3 6.5 %fusion.138 = (bf16[32,2,256,256]{2,3,0,1:T(8,128)(2,1)}, bf16[1,32,2,256,256]{3,4,1,2,0:T(8,128)(2,1)}) fusion(bf16[1,32,1,256,256]{3,4,1,2,0:T(8,128)(2,1)S(1)} %bitcast.415, bf16[1,32,1,256,256]{3,4,1,2,0:T(8,128)(2,1)S(1)} %bitcast.417), kind=kLoop, calls=%fused_computation.231 | loop fusion | flops 4194304 | bytes 25165824 | tf_op jit(solution)/shard_map/jit(_take)/Arg_0.3 | solution.py:61
  21.2 5.4 %collective-permute-start = (bf16[1,32,2,256,256]{3,4,1,2,0:T(8,128)(2,1)}, bf16[1,32,2,256,256]{3,4,1,2,0:T(8,128)(2,1)}, u32[]{:S(2)}, u32[]{:S(2)}) collective-permute-start(bf16[1,32,2,256,256]{3,4,1,2,0:T(8,128)(2,1)} %get-tuple-element.24), channel_id=1, source_target_pairs={{1,0},{2,1},{3,2},{4,3},{5,4},{6,5},{7,6},{8,7},{9,8},{10,9},{11,1... | collective-permute-start | bytes 25165832 | tf_op jit(solution)/shard_map/ppermute | solution.py:13
  26.7 6.5 %copy.261 = bf16[32,256,256]{2,1,0:T(8,128)(2,1)} copy(bf16[32,256,256]{1,2,0:T(8,128)(2,1)} %bitcast.418) | data formatting | bytes 8388608 | tf_op jit(solution)/shard_map/convert.7
  33.2 5.6 %stack.89 = bf16[32,1,65536]{2,0,1:T(8,128)(2,1)} reshape(bf16[32,256,256]{2,1,0:T(8,128)(2,1)} %copy.261) | data formatting | bytes 8388608 | tf_op jit(solution)/shard_map/stack | solution.py:92
  38.8 6.5 %copy.263 = bf16[32,256,256]{2,1,0:T(8,128)(2,1)} copy(bf16[32,256,256]{1,2,0:T(8,128)(2,1)} %bitcast.416) | data formatting | bytes 8388608 | tf_op jit(solution)/shard_map/convert.6
  45.2 5.7 %stack.91 = bf16[32,1,65536]{2,0,1:T(8,128)(2,1)} reshape(bf16[32,256,256]{2,1,0:T(8,128)(2,1)} %copy.263) | data formatting | bytes 8388608 | tf_op jit(solution)/shard_map/stack | solution.py:92
  50.9 5.4 %gather_fusion.3 = bf16[8,2,256,256]{2,3,1,0:T(8,128)(2,1)} fusion(bf16[32,2,256,256]{2,3,0,1:T(8,128)(2,1)} %get-tuple-element.23, s32[1024]{0:T(1024)S(1)} %pad_clamp_fusion), kind=kCustom, calls=%fused_computation.3.clone | custom fusion | bytes 4194336 | tf_op jit(solution)/shard_map/jit(_take)/gather | solution.py:64
  56.3 5.4 %gather_fusion = bf16[8,2,256,256]{2,3,1,0:T(8,128)(2,1)} fusion(bf16[32,2,256,256]{2,3,0,1:T(8,128)(2,1)} %get-tuple-element.23, s32[1024]{0:T(1024)S(1)} %pad_clamp_fusion.3), kind=kCustom, calls=%fused_computation.clone | custom fusion | bytes 4194336 | tf_op jit(solution)/shard_map/jit(_take)/gather | solution.py:61
  61.7 5.3 %gather_fusion.2 = bf16[8,2,256,256]{2,3,1,0:T(8,128)(2,1)} fusion(bf16[32,2,256,256]{2,3,0,1:T(8,128)(2,1)} %get-tuple-element.23, s32[1024]{0:T(1024)S(1)} %pad_clamp_fusion.1), kind=kCustom, calls=%fused_computation.2.clone | custom fusion | bytes 4194336 | tf_op jit(solution)/shard_map/jit(_take)/gather | solution.py:64
  67.1 5.4 %gather_fusion.1 = bf16[8,2,256,256]{2,3,1,0:T(8,128)(2,1)} fusion(bf16[32,2,256,256]{2,3,0,1:T(8,128)(2,1)} %get-tuple-element.23, s32[1024]{0:T(1024)S(1)} %pad_clamp_fusion.2), kind=kCustom, calls=%fused_computation.1.clone | custom fusion | bytes 4194336 | tf_op jit(solution)/shard_map/jit(_take)/gather | solution.py:61
  73.8 2.6 constant_dynamic-update-slice_fusion.1
  76.4 41.5 %collective-permute-done = bf16[1,32,2,256,256]{3,4,1,2,0:T(8,128)(2,1)} collective-permute-done((bf16[1,32,2,256,256]{3,4,1,2,0:T(8,128)(2,1)}, bf16[1,32,2,256,256]{3,4,1,2,0:T(8,128)(2,1)}, u32[]{:S(2)}, u32[]{:S(2)}) %collective-permute-start) | collective-permute-done | bytes 8388640 | tf_op jit(solution)/shard_map/ppermute | solution.py:13
  117.9 4.8 %collective-permute-start.1 = (bf16[1,32,2,256,256]{3,4,1,2,0:T(8,128)(2,1)}, bf16[1,32,2,256,256]{3,4,1,2,0:T(8,128)(2,1)}, u32[]{:S(2)}, u32[]{:S(2)}) collective-permute-start(bf16[1,32,2,256,256]{3,4,1,2,0:T(8,128)(2,1)} %collective-permute-done), channel_id=1, source_target_pairs={{1,0},{2,1},{3,2},{4,3},{5,4},{6,5},{7,6},{8,7},{9,8},{10,9},{11,1... | collective-permute-start | bytes 25165832 | tf_op jit(solution)/shard_map/ppermute | solution.py:13
  123.0 6.9 %fusion.69 = f32[1,32,2,32,2]{3,1,4,2,0:T(8,128)S(1)} fusion(bf16[32,2,65536]{2,0,1:T(8,128)(2,1)S(1)} %constant_dynamic-update-slice_fusion), kind=kOutput, calls=%fused_computation.117 | convolution fusion | flops 536870912 | bytes 8404992 | tf_op jit(solution)/shard_map/sam,sbm->sab/dot_general | solution.py:48
  131.8 5.4 %gather_fusion.5 = bf16[8,2,256,256]{2,3,1,0:T(8,128)(2,1)} fusion(bf16[32,2,256,256]{2,3,0,1:T(8,128)(2,1)} %bitcast.78, s32[1024]{0:T(1024)S(1)} %pad_clamp_fusion.1), kind=kCustom, calls=%fused_computation.5.clone | custom fusion | bytes 4194336 | tf_op jit(solution)/shard_map/jit(_take)/gather | solution.py:64
  137.2 5.4 %gather_fusion.4 = bf16[8,2,256,256]{2,3,1,0:T(8,128)(2,1)} fusion(bf16[32,2,256,256]{2,3,0,1:T(8,128)(2,1)} %bitcast.78, s32[1024]{0:T(1024)S(1)} %pad_clamp_fusion.2), kind=kCustom, calls=%fused_computation.4.clone | custom fusion | bytes 4194336 | tf_op jit(solution)/shard_map/jit(_take)/gather | solution.py:61
  142.6 12.3 %copy.279 = bf16[1,32,2,256,256]{4,3,1,2,0:T(8,128)(2,1)} copy(bf16[1,32,2,256,256]{3,4,1,2,0:T(8,128)(2,1)} %collective-permute-done) | data formatting | bytes 16777216 | tf_op jit(solution)/shard_map/ppermute | solution.py:13
  154.9 10.6 %reshape.774 = bf16[32,2,65536,1]{2,0,1,3:T(8,128)(2,1)} reshape(bf16[1,32,2,256,256]{4,3,1,2,0:T(8,128)(2,1)} %copy.279) | data formatting | bytes 16777216 | tf_op jit(solution)/shard_map/sam,sbm->sab/dot_general | solution.py:48
  165.5 9.3 %fusion.74 = f32[1,32,2,32,2]{3,1,4,2,0:T(8,128)S(1)} fusion(bf16[32,2,65536,1]{2,0,1,3:T(8,128)(2,1)} %reshape.774, bf16[32,2,65536]{2,0,1:T(8,128)(2,1)} %copy-done.21), kind=kOutput, calls=%fused_computation.118 | convolution fusion | flops 536870912 | bytes 16793600 | tf_op jit(solution)/shard_map/sam,sbm->sab/dot_general | solution.py:48
  176.7 37.3 %collective-permute-done.1 = bf16[1,32,2,256,256]{3,4,1,2,0:T(8,128)(2,1)} collective-permute-done((bf16[1,32,2,256,256]{3,4,1,2,0:T(8,128)(2,1)}, bf16[1,32,2,256,256]{3,4,1,2,0:T(8,128)(2,1)}, u32[]{:S(2)}, u32[]{:S(2)}) %collective-permute-start.1) | collective-permute-done | bytes 8388640 | tf_op jit(solution)/shard_map/ppermute | solution.py:13
  214.0 5.5 %gather_fusion.7 = bf16[8,2,256,256]{2,3,1,0:T(8,128)(2,1)} fusion(bf16[32,2,256,256]{2,3,0,1:T(8,128)(2,1)} %bitcast.109, s32[1024]{0:T(1024)S(1)} %pad_clamp_fusion.1), kind=kCustom, calls=%fused_computation.7.clone | custom fusion | bytes 4194336 | tf_op jit(solution)/shard_map/jit(_take)/gather | solution.py:64
  219.5 5.4 %gather_fusion.6 = bf16[8,2,256,256]{2,3,1,0:T(8,128)(2,1)} fusion(bf16[32,2,256,256]{2,3,0,1:T(8,128)(2,1)} %bitcast.109, s32[1024]{0:T(1024)S(1)} %pad_clamp_fusion.2), kind=kCustom, calls=%fused_computation.6.clone | custom fusion | bytes 4194336 | tf_op jit(solution)/shard_map/jit(_take)/gather | solution.py:61
  224.9 4.3 bitcast_select_fusion.6
  229.2 2.2 fusion.85
  231.3 2.1 fusion.52
  233.5 1.8 fusion.83
  235.3 2.2 fusion.41
  237.5 1.8 fusion.81
  239.3 2.2 fusion.33
  241.5 11.9 %copy.295 = bf16[1,32,2,256,256]{4,3,1,2,0:T(8,128)(2,1)} copy(bf16[1,32,2,256,256]{3,4,1,2,0:T(8,128)(2,1)} %collective-permute-done.1) | data formatting | bytes 16777216 | tf_op jit(solution)/shard_map/ppermute | solution.py:13
  253.4 10.6 %reshape.777 = bf16[32,2,65536,1]{2,0,1,3:T(8,128)(2,1)} reshape(bf16[1,32,2,256,256]{4,3,1,2,0:T(8,128)(2,1)} %copy.295) | data formatting | bytes 16777216 | tf_op jit(solution)/shard_map/sam,sbm->sab/dot_general | solution.py:48
  264.0 9.6 %fusion.77 = f32[1,32,2,32,2]{3,1,4,2,0:T(8,128)S(1)} fusion(bf16[32,2,65536,1]{2,0,1,3:T(8,128)(2,1)} %reshape.777, bf16[32,2,65536]{2,0,1:T(8,128)(2,1)} %copy-done.21), kind=kOutput, calls=%fused_computation.119 | convolution fusion | flops 536870912 | bytes 16793600 | tf_op jit(solution)/shard_map/sam,sbm->sab/dot_general | solution.py:48
  275.5 1.8 convolution_subtract_fusion.5
  277.4 1.1 copy-done.13
  278.5 1.9 convolution_subtract_fusion.3
  281.5 1.8 convolution_subtract_fusion.1
  283.3 1.1 copy-done.10
  285.1 2.4 bitcast_select_fusion.5
  292.2 1.3 fusion.44
  294.5 1.3 fusion.36
  296.7 1.3 fusion.28
  301.4 2.0 copy.280
  303.4 22.7 %scatter_custom_fusion.4 = f32[64,2]{1,0:T(8,128)S(1)} fusion(s32[4096]{0:T(1024)} %param.14, f32[4096,2]{1,0:T(8,128)S(1)} %copy.296, f32[]{:T(128)} %constant.26.clone.1), kind=kCustom, calls=%fused_computation.192 | custom fusion | flops 8192 | bytes 1024 | tf_op jit(solution)/shard_map/scatter-add | solution.py:72
  326.1 22.7 %scatter_custom_fusion.2 = f32[64,2]{1,0:T(8,128)S(1)} fusion(s32[4096]{0:T(1024)} %param.14, f32[4096,2]{1,0:T(8,128)} %copy.280, f32[]{:T(128)} %constant.26.clone.1), kind=kCustom, calls=%fused_computation.196 | custom fusion | flops 8192 | bytes 1024 | tf_op jit(solution)/shard_map/scatter-add | solution.py:72
  349.5 22.5 %scatter_custom_fusion = f32[64,2]{1,0:T(8,128)S(1)} fusion(s32[4096]{0:T(1024)} %param.14, f32[4096,2]{1,0:T(8,128)S(1)} %copy.264, f32[]{:T(128)} %constant.26.clone.1), kind=kCustom, calls=%fused_computation.200 | custom fusion | flops 8192 | bytes 1024 | tf_op jit(solution)/shard_map/scatter-add | solution.py:72
  372.0 63.0 %all-reduce.3 = (f32[2,64]{0,1:T(8,128)S(1)}, f32[2,64]{0,1:T(8,128)S(1)}, f32[2,64]{0,1:T(8,128)S(1)}) all-reduce(f32[2,64]{0,1:T(8,128)S(1)} %subtract_bitcast_fusion, f32[2,64]{0,1:T(8,128)S(1)} %subtract_bitcast_fusion.1, f32[2,64]{0,1:T(8,128)S(1)} %subtract_bitcast_fusion.2), channel_id=4, replica_groups=mesh['cfg'=2,'tm'=16] {'tm'}, use_global_device_ids=true, to_apply=%region_26.28.clone | all-reduce | flops 384 | bytes 3072
  (108 shorter events, 21.2 us)
Async XLA Ops:
  7.0 7.3 %copy-start.7 = (bf16[256,32,256]{2,0,1:T(8,128)(2,1)}, bf16[256,32,256]{2,0,1:T(8,128)(2,1)S(1)}, u32[]{:S(2)}) copy-start(bf16[256,32,256]{2,0,1:T(8,128)(2,1)S(1)} %bitcast_convert_fusion) | copy-start | bytes 12582916
  14.3 6.9 %copy-start.8 = (bf16[256,32,256]{2,0,1:T(8,128)(2,1)}, bf16[256,32,256]{2,0,1:T(8,128)(2,1)S(1)}, u32[]{:S(2)}) copy-start(bf16[256,32,256]{2,0,1:T(8,128)(2,1)S(1)} %bitcast_convert_fusion.1) | copy-start | bytes 12582916
  14.3 12.3 %copy-start.24 = (s32[8,4]{0,1:T(4,128)S(1)}, s32[8,4]{0,1:T(4,128)}, u32[]{:S(2)}) copy-start(s32[8,4]{0,1:T(4,128)} %param.15) | copy-start | bytes 388
  21.2 96.7 %collective-permute-start = (bf16[1,32,2,256,256]{3,4,1,2,0:T(8,128)(2,1)}, bf16[1,32,2,256,256]{3,4,1,2,0:T(8,128)(2,1)}, u32[]{:S(2)}, u32[]{:S(2)}) collective-permute-start(bf16[1,32,2,256,256]{3,4,1,2,0:T(8,128)(2,1)} %get-tuple-element.24), channel_id=1, source_target_pairs={{1,0},{2,1},{3,2},{4,3},{5,4},{6,5},{7,6},{8,7},{9,8},{10,9},{11,1... | collective-permute-start | bytes 25165832 | tf_op jit(solution)/shard_map/ppermute | solution.py:13
  67.0 5.4 %copy-start.26 = (u32[32]{0:T(128)S(1)}, u32[32]{0:T(128)}, u32[]{:S(2)}) copy-start(u32[32]{0:T(128)} %constant.32) | copy-start | bytes 388
  67.0 6.7 %copy-start.22 = (s32[4096,4]{0,1:T(4,128)S(1)}, s32[4096,4]{0,1:T(4,128)}, u32[]{:S(2)}) copy-start(s32[4096,4]{0,1:T(4,128)} %param.12) | copy-start | bytes 196612
  73.8 49.0 %copy-start.6 = (bf16[32,1,65536]{2,0,1:T(8,128)(2,1)S(1)}, bf16[32,1,65536]{2,0,1:T(8,128)(2,1)}, u32[]{:S(2)}) copy-start(bf16[32,1,65536]{2,0,1:T(8,128)(2,1)} %stack.91) | copy-start | bytes 12582916
  117.9 96.1 %collective-permute-start.1 = (bf16[1,32,2,256,256]{3,4,1,2,0:T(8,128)(2,1)}, bf16[1,32,2,256,256]{3,4,1,2,0:T(8,128)(2,1)}, u32[]{:S(2)}, u32[]{:S(2)}) collective-permute-start(bf16[1,32,2,256,256]{3,4,1,2,0:T(8,128)(2,1)} %collective-permute-done), channel_id=1, source_target_pairs={{1,0},{2,1},{3,2},{4,3},{5,4},{6,5},{7,6},{8,7},{9,8},{10,9},{11,1... | collective-permute-start | bytes 25165832 | tf_op jit(solution)/shard_map/ppermute | solution.py:13
  123.0 6.9 %copy-start.21 = (bf16[32,2,65536]{2,0,1:T(8,128)(2,1)}, bf16[32,2,65536]{2,0,1:T(8,128)(2,1)S(1)}, u32[]{:S(2)}) copy-start(bf16[32,2,65536]{2,0,1:T(8,128)(2,1)S(1)} %constant_dynamic-update-slice_fusion) | copy-start | bytes 25165828
  229.1 6.2 %copy-start.2 = (bf16[1,8,2,256,256]{3,4,2,1,0:T(8,128)(2,1)}, bf16[1,8,2,256,256]{3,4,2,1,0:T(8,128)(2,1)S(1)}, u32[]{:S(2)}) copy-start(bf16[1,8,2,256,256]{3,4,2,1,0:T(8,128)(2,1)S(1)} %get-tuple-element.54) | copy-start | bytes 6291460
  229.1 6.2 %copy-start.4 = (bf16[1,8,2,256,256]{3,4,2,1,0:T(8,128)(2,1)}, bf16[1,8,2,256,256]{3,4,2,1,0:T(8,128)(2,1)S(1)}, u32[]{:S(2)}) copy-start(bf16[1,8,2,256,256]{3,4,2,1,0:T(8,128)(2,1)S(1)} %get-tuple-element.53) | copy-start | bytes 6291460
  229.1 10.2 %copy-start = (bf16[1,8,2,256,256]{3,4,2,1,0:T(8,128)(2,1)}, bf16[1,8,2,256,256]{3,4,2,1,0:T(8,128)(2,1)S(1)}, u32[]{:S(2)}) copy-start(bf16[1,8,2,256,256]{3,4,2,1,0:T(8,128)(2,1)S(1)} %get-tuple-element.55) | copy-start | bytes 6291460
  264.0 11.5 %copy-start.5 = (bf16[1,8,2,256,256]{3,4,2,1,0:T(8,128)(2,1)S(1)}, bf16[1,8,2,256,256]{3,4,2,1,0:T(8,128)(2,1)}, u32[]{:S(2)}) copy-start(bf16[1,8,2,256,256]{3,4,2,1,0:T(8,128)(2,1)} %copy-done.4) | copy-start | bytes 6291460
  264.0 11.5 %copy-start.14 = (f32[8,256,256]{2,1,0:T(8,128)S(1)}, f32[8,256,256]{2,1,0:T(8,128)}, u32[]{:S(2)}) copy-start(f32[8,256,256]{2,1,0:T(8,128)} %fusion.85) | copy-start | bytes 6291460
  275.5 1.9 copy-start.3
  275.5 3.0 copy-start.13
  278.5 1.9 copy-start.1
  278.5 3.0 copy-start.12
  281.5 1.8 copy-start.9
  281.5 3.0 copy-start.10
  281.5 3.6 copy-start.11
  290.0 1.6 copy-start.17
  290.0 2.2 copy-start.20
  292.2 1.6 copy-start.16
  292.2 2.2 copy-start.19
  294.5 1.6 copy-start.15
  294.5 2.2 copy-start.18
  296.7 1.3 copy-start.25
  296.7 4.0 copy-start.23
where the time goes:
time: 444 us; the launch traced here: 436 us
  local copies, waits for them, and re-layouts  129 us (29%)
  other arithmetic  84.1 us (19%)
  waiting for transfers between devices  78.9 us (18%)
  matrix products  69.2 us (16%)
  blocking collectives  63 us (14%)
  starting transfers between devices  10.2 us (2%)
    ppermute x2, waiting for transfers between devices, from_behind(): return lax.ppermute(block, axis, route)  78.9 us
    scatter-add x3, other arithmetic, pair_terms(): jax.ops.segment_sum(jnp.stack([direct_real, direct_imag], 1), direct_entr...  67.8 us
    unnamed x1, blocking collectives  63 us
    dot_general x3, matrix products, pair_terms(): jnp.einsum('sam,sbm->sab', sink_rows, source_rows, preferred_element_type...  25.8 us
    ppermute x2, local copies, waits for them, and re-layouts, from_behind(): return lax.ppermute(block, axis, route)  24.3 us
    dot_general x2, local copies, waits for them, and re-layouts, pair_terms(): jnp.einsum('sam,sbm->sab', sink_rows, source_rows, preferred_element_type...  21.1 us
    gather x3, local copies, waits for them, and re-layouts, pair_terms(): jnp.take(source, box_ins[:, 1], axis=1)  16.2 us
    gather x3, local copies, waits for them, and re-layouts, pair_terms(): jnp.take(source, box_ins[:, 3], axis=1)  16.2 us
  transfers between devices with their start and end apart: 2, of which 2 were waited for; matrix products, arithmetic and copies ran while one was open for 24% of the time, Pallas kernels for 0%

commit v1 on v0

v1 whole, which is shorter than its diff:
```python
import functools

import jax
import jax.numpy as jnp
from jax import lax
from jax.experimental import pallas as pl
from jax.experimental.pallas import tpu as pltpu
from jax.sharding import PartitionSpec as P

GROUP = 4
SEPARATIONS = 3
SLOTS = GROUP + SEPARATIONS - 1
MESH = pl.DeviceIdType.MESH
HIGHEST = lax.Precision.HIGHEST


def dress_kernel(fields, taus, out):
    count, rows = fields.shape[1], fields.shape[2]
    left = fields[0].reshape(count * rows, rows)
    right = fields[1].reshape(count * rows, rows)
    both = jnp.dot(left, taus[0], preferred_element_type=jnp.float32)
    both += jnp.dot(right, taus[1], preferred_element_type=jnp.float32)
    both = both.astype(jnp.bfloat16).reshape(count, GROUP, rows // GROUP, 2 * rows)
    for quarter in range(GROUP):
        for part in range(2):
            out[quarter, :, part] = both[:, quarter, :, part * rows : (part + 1) * rows]


def dress(fields, perambulators, block):
    _, inserts, modes, _ = fields.shape
    real_row = jnp.concatenate([perambulators[0], perambulators[1]], 1)
    imag_row = jnp.concatenate([-perambulators[1], perambulators[0]], 1)
    taus = jnp.stack([real_row, imag_row])
    return pl.pallas_call(
        dress_kernel,
        grid=(inserts // block,),
        in_specs=[
            pl.BlockSpec((2, block, modes, modes), lambda g: (0, g, 0, 0)),
            pl.BlockSpec((2, modes, 2 * modes), lambda g: (0, 0, 0)),
        ],
        out_specs=pl.BlockSpec((GROUP, block, 2, modes // GROUP, modes), lambda g: (0, g, 0, 0, 0)),
        out_shape=jax.ShapeDtypeStruct((GROUP, inserts, 2, modes // GROUP, modes), jnp.bfloat16),
        compiler_params=pltpu.CompilerParams(vmem_limit_bytes=40 * 2**20),
    )(fields, taus)


def missing_quarters(owner):
    far = 2 - 2 * (owner // 2)
    return (far, far + 1, owner + 1 - 2 * (owner % 2))


def pick_kernel(each, index, source, out):
    owner = pl.program_id(0) // each
    for place, quarter in enumerate(missing_quarters(owner)):
        out[0, 0, place] = source[quarter, 0]


def pick(quarters, index):
    total = index.shape[0]
    each = total // GROUP
    _, _, _, rows, modes = quarters.shape
    return pl.pallas_call(
        functools.partial(pick_kernel, each),
        grid_spec=pltpu.PrefetchScalarGridSpec(
            num_scalar_prefetch=1,
            grid=(total,),
            in_specs=[pl.BlockSpec((GROUP, 1, 2, rows, modes), lambda e, index: (0, index[e], 0, 0, 0))],
            out_specs=pl.BlockSpec(
                (1, 1, 3, 2, rows, modes), lambda e, index: (e // each, e % each, 0, 0, 0, 0)
            ),
        ),
        out_shape=jax.ShapeDtypeStruct((GROUP, each, 3, 2, rows, modes), jnp.bfloat16),
    )(index, quarters)


def other(rank, step):
    if step == 1:
        return rank + 1 - 2 * (rank % 2)
    if step == 2:
        return (rank + 2) % GROUP
    return GROUP - 1 - rank


def slot_of(rank, side):
    return rank + side * (GROUP - 1 - 2 * rank)


def exchange_kernel(n, lines, boxes, line_slots, box_slots, send_sem, recv_sem, local_sem):
    me = lax.axis_index("tm")
    rank = me % GROUP
    base = me - rank
    side = rank // 2
    half = boxes.shape[1] // 2
    target = (base + n - GROUP + 2 * side * GROUP) % n
    origin = (base + n + GROUP - 2 * side * GROUP) % n
    peers = [other(rank, step) for step in (2, 3, 1)]

    barrier = pltpu.get_barrier_semaphore()
    near = [base + peer for peer in peers]
    far = [group + 2 * side + core for group in (target, origin) for core in range(2)]
    for device in near + far:
        pl.semaphore_signal(barrier, inc=1, device_id={"tm": device}, device_id_type=MESH)
    pl.semaphore_wait(barrier, len(near) + len(far))

    def copies(order, owner, device, slot, whole):
        box_from, box_to = boxes.at[owner], box_slots.at[slot]
        if not whole:
            box_from, box_to = box_from.at[pl.ds(half, half)], box_to.at[pl.ds(half, half)]
        return [
            pltpu.make_async_remote_copy(
                src_ref=source,
                dst_ref=landing,
                send_sem=send_sem.at[order, kind],
                recv_sem=recv_sem.at[slot, kind],
                device_id={"tm": device},
                device_id_type=MESH,
            )
            for kind, (source, landing) in enumerate(
                ((lines.at[owner], line_slots.at[slot]), (box_from, box_to))
            )
        ]

    sent = []
    for order, peer in enumerate(peers):
        sent += copies(order, peer, base + peer, slot_of(rank, peer // 2), True)
        for copy in sent[-2:]:
            copy.start()
        if order < 2:
            owner = 2 * side + (rank + order) % 2
            sent += copies(3 + order, owner, target + owner, GROUP + slot_of(rank, side), False)
            for copy in sent[-2:]:
                copy.start()
    own = slot_of(rank, side)
    kept = [
        pltpu.make_async_copy(lines.at[rank], line_slots.at[own], local_sem.at[0]),
        pltpu.make_async_copy(boxes.at[rank], box_slots.at[own], local_sem.at[1]),
    ]
    for copy in kept:
        copy.start()
    for copy in kept:
        copy.wait()
    for copy in sent:
        copy.wait_send()
    for peer in peers:
        for copy in copies(0, rank, me, slot_of(peer, side), True):
            copy.wait_recv()
    for place in range(2):
        for copy in copies(0, rank, me, GROUP + place, False):
            copy.wait_recv()


def exchange(n, lines, boxes):
    return pl.pallas_call(
        functools.partial(exchange_kernel, n),
        in_specs=[pl.BlockSpec(memory_space=pl.ANY)] * 2,
        out_specs=[pl.BlockSpec(memory_space=pl.ANY)] * 2,
        out_shape=[
            jax.ShapeDtypeStruct((SLOTS, *lines.shape[1:]), jnp.bfloat16),
            jax.ShapeDtypeStruct((SLOTS, *boxes.shape[1:]), jnp.bfloat16),
        ],
        scratch_shapes=[
            pltpu.SemaphoreType.DMA((5, 2)),
            pltpu.SemaphoreType.DMA((SLOTS, 2)),
            pltpu.SemaphoreType.DMA((2,)),
        ],
        compiler_params=pltpu.CompilerParams(
            collective_id=0, has_side_effects=True, vmem_limit_bytes=2**20
        ),
    )(lines, boxes)


def pairs_kernel(terms, index, where, line, box, gram, traces, flat, plain, turned):
    slot = pl.program_id(0)
    inserts, _, rows, modes = line.shape[1:]
    owner = where[0]
    side = owner // 2
    each = 4 * terms

    @pl.when(slot == 0)
    def _():
        traces[...] = jnp.zeros_like(traces)

    step = 16
    for start in range(0, rows, step):
        block = line[0, :, :, start : start + step, :].reshape(2 * inserts, step, modes)
        flat[slot, :, start * modes : (start + step) * modes] = block.reshape(2 * inserts, step * modes)

    quarters = missing_quarters(owner)
    for entry in range(each):
        role, rest = divmod(entry, 2 * terms)
        term, which = divmod(rest, 2)
        spot = (role * terms + term) * 2 + which
        is_left = role == which

        def fill(quarter, values):
            at = pl.ds(pl.multiple_of(quarter * rows, rows), rows)
            real, imag = values
            plain[slot, spot, at, :modes] = real
            plain[slot, spot, at, modes:] = imag
            if is_left:
                spun = role * terms + term
                turned[slot, spun, at, :modes] = imag
                turned[slot, spun, at, modes:] = -real

        for place, quarter in enumerate(quarters):
            fill(quarter, (box[0, entry, place, 0], box[0, entry, place, 1]))
        ins = index[owner * each + entry]
        fill(owner, (line[0, ins, 0], line[0, ins, 1]))

    contract = (((1,), (1,)), ((), ()))
    for k in range(SEPARATIONS):
        sink = slot - k

        @pl.when((sink >= 0) & (sink < GROUP))
        def _(k=k, sink=sink):
            gram[sink, k] = lax.dot_general(
                flat[sink], flat[slot], contract, preferred_element_type=jnp.float32
            )
            for term in range(terms):
                a, a_turned = plain[sink, 2 * term], turned[sink, term]
                c = plain[sink, 2 * term + 1]
                b = plain[slot, 2 * terms + 2 * term]
                e, e_turned = plain[slot, 2 * terms + 2 * term + 1], turned[slot, terms + term]
                first_real = lax.dot_general(a, b, contract, preferred_element_type=jnp.float32)
                first_imag = lax.dot_general(a_turned, b, contract, preferred_element_type=jnp.float32)
                second_real = lax.dot_general(e, c, contract, preferred_element_type=jnp.float32)
                second_imag = lax.dot_general(e_turned, c, contract, preferred_element_type=jnp.float32)
                real = first_real * second_real + first_imag * second_imag
                imag = first_imag * second_real - first_real * second_imag
                for part, value in enumerate((real, imag)):
                    traces[k, term, part] += jnp.sum(value.reshape(-1, 8, modes), axis=0)


def pairs(index, rank, line_slots, box_slots):
    _, inserts, _, rows, modes = line_slots.shape
    each = box_slots.shape[1]
    terms = each // 4
    return pl.pallas_call(
        functools.partial(pairs_kernel, terms),
        grid_spec=pltpu.PrefetchScalarGridSpec(
            num_scalar_prefetch=2,
            grid=(SLOTS,),
            in_specs=[
                pl.BlockSpec((1, inserts, 2, rows, modes), lambda s, *_: (s, 0, 0, 0, 0)),
                pl.BlockSpec((1, each, 3, 2, rows, modes), lambda s, *_: (s, 0, 0, 0, 0, 0)),
            ],
            out_specs=[
                pl.BlockSpec((GROUP, SEPARATIONS, 2 * inserts, 2 * inserts), lambda s, *_: (0, 0, 0, 0)),
                pl.BlockSpec((SEPARATIONS, terms, 2, 8, modes), lambda s, *_: (0, 0, 0, 0, 0)),
            ],
            scratch_shapes=[
                pltpu.VMEM((SLOTS, 2 * inserts, rows * modes), jnp.bfloat16),
                pltpu.VMEM((SLOTS, each, modes, 2 * modes), jnp.bfloat16),
                pltpu.VMEM((SLOTS, 2 * terms, modes, 2 * modes), jnp.bfloat16),
            ],
        ),
        out_shape=[
            jax.ShapeDtypeStruct((GROUP, SEPARATIONS, 2 * inserts, 2 * inserts), jnp.float32),
            jax.ShapeDtypeStruct((SEPARATIONS, terms, 2, 8, modes), jnp.float32),
        ],
        compiler_params=pltpu.CompilerParams(vmem_limit_bytes=56 * 2**20),
    )(index, rank[None], line_slots, box_slots)


def local(
    entries,
    meson_fields,
    perambulators,
    direct_ins,
    direct_coef,
    direct_entry,
    box_ins,
    box_coef,
    box_entry,
):
    n = lax.axis_size("tm")
    me = lax.axis_index("tm")
    rank = me % GROUP
    base = me - rank
    right = rank >= 2
    inserts = meson_fields.shape[1]
    terms = box_ins.shape[0] // GROUP

    by_owner = box_ins.reshape(GROUP, terms, 4)
    by_owner = jnp.concatenate([by_owner[:2], by_owner[2:, :, ::-1]], 0)
    index = jnp.transpose(by_owner.reshape(GROUP, terms, 2, 2), (0, 3, 1, 2)).reshape(-1)

    lines = dress(meson_fields[:, :, 0], perambulators[:, 0], 4)
    boxes = pick(lines, index)
    line_slots, box_slots = exchange(n, lines, boxes)
    gram, traces = pairs(index, rank, line_slots, box_slots)

    gram = gram.reshape(GROUP, SEPARATIONS, inserts, 2, inserts, 2)
    loop_real = gram[:, :, :, 0, :, 0] + gram[:, :, :, 1, :, 1]
    loop_imag = gram[:, :, :, 1, :, 0] - gram[:, :, :, 0, :, 1]
    parts = jnp.stack([loop_real, loop_imag], 2)
    flipped = jnp.stack([jnp.swapaxes(loop_real, 2, 3), -jnp.swapaxes(loop_imag, 2, 3)], 2)
    parts = jnp.where(right, flipped, parts)
    slot = jnp.arange(GROUP, dtype=jnp.int32)[:, None]
    apart = jnp.arange(SEPARATIONS, dtype=jnp.int32)[None]
    sink_time = jnp.where(right, base + GROUP - 1 - slot - apart, base + slot) % n
    hot = (sink_time[..., None] == jnp.arange(n, dtype=jnp.int32)).astype(jnp.float32)
    spread = jnp.sum(hot[..., None, None, None] * parts[:, :, None], axis=0)
    spread = jnp.transpose(spread, (1, 0, 2, 3, 4))
    loops = lax.psum_scatter(spread, "tm", scatter_dimension=0, tiled=True)[0]

    inserted = jnp.arange(inserts, dtype=jnp.int32)[:, None]
    hots = [(direct_ins[:, p][None] == inserted).astype(jnp.float32) for p in range(4)]

    def lookup(row_hot, column_hot):
        picked = jnp.einsum("kcab,al->kcbl", loops, row_hot, precision=HIGHEST)
        return jnp.sum(picked * column_hot, axis=2)

    left, second = lookup(hots[0], hots[1]), lookup(hots[2], hots[3])
    direct_real = left[:, 0] * second[:, 0] - left[:, 1] * second[:, 1]
    direct_imag = left[:, 0] * second[:, 1] + left[:, 1] * second[:, 0]
    direct = direct_coef * jnp.stack([direct_real, direct_imag], 1)
    entry_hot = (direct_entry[:, None] == jnp.arange(entries, dtype=jnp.int32)).astype(jnp.float32)
    direct_sum = jnp.einsum("kcl,le->kce", direct, entry_hot, precision=HIGHEST)

    traces = jnp.sum(traces, axis=(3, 4))
    sign = jnp.stack([jnp.float32(1), jnp.where(right, -1.0, 1.0).astype(jnp.float32)])
    coef = lax.dynamic_slice(box_coef, (rank * terms,), (terms,))
    entry = lax.dynamic_slice(box_entry, (rank * terms,), (terms,))
    box_hot = (entry[:, None] == jnp.arange(entries, dtype=jnp.int32)).astype(jnp.float32)
    weighted = traces * coef[None, :, None] * sign
    box_sum = jnp.sum(weighted[..., None] * box_hot[None, :, None], axis=1)

    total = lax.psum_scatter(direct_sum - box_sum, "tm", scatter_dimension=2, tiled=True)
    return total / n


ENTRY_DEV = 4


def solution(mesh):
    placed = (
        P(None, None, ("cfg", "tm"), None, None),
        P(None, ("cfg", "tm"), None, None),
        P(),
        P(),
        P(),
        P(),
        P(),
        P(),
    )
    entries = ENTRY_DEV * mesh.shape["tm"]
    return jax.shard_map(
        functools.partial(local, entries),
        mesh=mesh,
        in_specs=placed,
        out_specs=P(None, None, ("cfg", "tm")),
        check_vma=False,
    )
```

time: 444 us -> 407 us (0.917); the launches traced: 436 us -> 405 us
  Pallas kernels: 0 us -> 216 us
  local copies, waits for them, and re-layouts: 129 us -> 32.8 us
  other arithmetic: 84.1 us -> 13.4 us
  matrix products: 69.2 us -> 7.09 us
  blocking collectives: 63 us -> 30.2 us
  between operations: 1.47 us -> 14.2 us
  waiting for transfers between devices: 78.9 us -> 91.2 us
  starting transfers between devices: 10.2 us -> 0.01 us
    pallas_call x0 -> x4, Pallas kernels: none -> 216 us  [the longest x1 165 us: exchange(): pl.pallas_call(functools.partial(exchange_kernel, n), in_specs=[pl.BlockS...]
    unnamed x0 -> x2, waiting for transfers between devices: none -> 91.2 us
    ppermute x2 -> x0, waiting for transfers between devices: 78.9 us -> none  [from_behind(): return lax.ppermute(block, axis, route)]
    scatter-add x6 -> x0, other arithmetic: 70.1 us -> none  [the longest x3 67.8 us: pair_terms(): jax.ops.segment_sum(jnp.stack([direct_real, direct_imag], 1), direct_entr...]
    dot_general x35 -> x3, matrix products: 69.2 us -> 7.09 us  [the longest x2 6.35 us: lookup(): picked = jnp.einsum('kcab,al->kcbl', loops, row_hot, precision=HIGHEST)]
    gather x8 -> x0, local copies, waits for them, and re-layouts: 43.2 us -> none  [the longest x3 16.2 us: pair_terms(): jnp.take(source, box_ins[:, 1], axis=1)]
    unnamed x1, blocking collectives: 63 us -> 30.2 us
    another operation x11 -> x2, local copies, waits for them, and re-layouts: 28 us -> 3.16 us  [local(): jnp.stack([jnp.swapaxes(loop_real, 2, 3), -jnp.swapaxes(loop_imag, 2, 3)]...]
  transfers between devices with their start and end apart: 2 -> 1, of which waited for: 2 -> 1; matrix products, arithmetic and copies ran while one was open for 24% -> 0% of each run, Pallas kernels for 0% -> 0%
where the time goes in v1:
time: 407 us; the launch traced here: 405 us
  Pallas kernels  216 us (53%)
  waiting for transfers between devices  91.2 us (22%)
  local copies, waits for them, and re-layouts  32.8 us (8%)
  blocking collectives  30.2 us (7%)
  between operations  14.2 us (3%)
  other arithmetic  13.4 us (3%)
  matrix products  7.09 us (2%)
    pallas_call x1, Pallas kernels, exchange(): pl.pallas_call(functools.partial(exchange_kernel, n), in_specs=[pl.BlockS...  165 us
    unnamed x2, waiting for transfers between devices  91.2 us
    unnamed x1, blocking collectives  30.2 us
    pallas_call x1, Pallas kernels, pairs(): pl.pallas_call(functools.partial(pairs_kernel, terms), grid_spec=pltpu.Pr...  23.4 us
    pallas_call x1, Pallas kernels, pick(): pl.pallas_call(functools.partial(pick_kernel, each), grid_spec=pltpu.Pref...  19.5 us
    unnamed x27, local copies, waits for them, and re-layouts  18.6 us
    neg x1, other arithmetic, local(): -jnp.swapaxes(loop_imag, 2, 3)  9.6 us
    pallas_call x1, Pallas kernels, dress(): pl.pallas_call(dress_kernel, grid=(inserts // block,), in_specs=[pl.Block...  9 us
  transfers between devices with their start and end apart: 1, of which 1 were waited for; matrix products, arithmetic and copies ran while one was open for 0% of the time, Pallas kernels for 0%

profile of v1, /device:TPU:0, one launch (start us, length us, event | category | flops | bytes accessed | tf_op | source)
XLA Modules:
  0.0 405.4 jit_solution(11213329620610784890)
XLA Ops:
  6.5 1.0 slice_bitcast_fusion
  7.5 0.9 fusion.21
  8.4 0.8 fusion.24
  9.3 0.1 copy.54
  9.4 0.1 rev.3
  9.5 0.1 concatenate.23
  9.6 0.1 copy.53
  9.6 0.1 concatenate.22
  9.7 0.1 copy.55
  9.9 0.7 reshape.230.index
  10.6 0.1 pad_maximum_fusion.taus
  10.6 9.0 %shard_map.82.source.lines = bf16[4,32,2,64,256]{4,3,2,1,0:T(8,128)(2,1)S(1)} custom-call(bf16[2,32,256,256]{3,2,1,0:T(8,128)(2,1)} %bitcast.63, bf16[2,256,512]{2,1,0:T(8,128)(2,1)S(1)} %pad_maximum_fusion.taus), custom_call_target="tpu_custom_call" | custom-call | tf_op jit(solution)/shard_map/pallas_call | solution.py:34
  19.7 3.2 copy-done
  22.9 19.5 %shard_map.83.boxes = bf16[4,8,3,2,64,256]{5,4,3,2,1,0:T(8,128)(2,1)} custom-call(s32[32]{0:T(128)} %reshape.230.index, bf16[4,32,2,64,256]{4,3,2,1,0:T(8,128)(2,1)} %copy-done), custom_call_target="tpu_custom_call" | custom-call | tf_op jit(solution)/shard_map/pallas_call | solution.py:62
  42.4 3.4 copy-done.1
  45.8 2.8 copy-done.2
  48.6 164.6 %shard_map.84 = (bf16[6,32,2,64,256]{4,3,2,1,0:T(8,128)(2,1)S(1)}, bf16[6,8,3,2,64,256]{5,4,3,2,1,0:T(8,128)(2,1)S(1)}) custom-call(bf16[4,32,2,64,256]{4,3,2,1,0:T(8,128)(2,1)S(1)} %copy-done.1, bf16[4,8,3,2,64,256]{5,4,3,2,1,0:T(8,128)(2,1)S(1)} %copy-done.2), custom_call_target="tpu_custom_call" | custom-call | tf_op jit(solution)/shard_map/pallas_call | solution.py:153
  213.2 4.5 %copy-done.3 = bf16[6,32,2,64,256]{4,3,2,1,0:T(8,128)(2,1)} copy-done((bf16[6,32,2,64,256]{4,3,2,1,0:T(8,128)(2,1)}, bf16[6,32,2,64,256]{4,3,2,1,0:T(8,128)(2,1)S(1)}, u32[]{:S(2)}) %copy-start.3) | copy-done | bytes 12582936
  217.7 3.5 copy-done.4
  221.2 23.4 %shard_map.85 = (f32[4,3,64,64]{3,2,1,0:T(8,128)}, f32[3,2,2,8,256]{4,3,2,1,0:T(8,128)}) custom-call(s32[32]{0:T(128)} %reshape.230.index, s32[1]{0:T(128)} %bitcast.2.where, bf16[6,32,2,64,256]{4,3,2,1,0:T(8,128)(2,1)} %copy-done.3, bf16[6,8,3,2,64,256]{5,4,3,2,1,0:T(8,128)(2,1)} %copy-done.4), custom_call_target="tpu_custom_call" | custom-call | tf_op jit(solution)/shard_map/pallas_call | solution.py:238
  244.6 5.0 %copy.56 = f32[4,3,64,64]{0,3,2,1:T(8,128)} copy(f32[4,3,64,64]{3,2,1,0:T(8,128)} %get-tuple-element.11) | data formatting | bytes 393216 | tf_op jit(solution)/shard_map/pallas_call | solution.py:238
  249.6 9.6 %fusion.22 = (f32[4,3,32,1,32,1]{0,5,4,3,2,1:T(1,128)}, f32[4,3,32,1,32,1]{0,5,4,3,2,1:T(1,128)S(1)}, f32[4,3,32,1,32,1]{0,5,4,3,2,1:T(1,128)S(1)}) fusion(f32[4,3,32,2,32,2]{0,5,4,3,2,1:T(2,128)} %bitcast.60), kind=kLoop, calls=%fused_computation.52 | loop fusion | flops 36864 | bytes 344064 | tf_op jit(solution)/shard_map/neg | solution.py:297
  259.2 0.9 copy.57
  260.1 2.2 copy.58
  262.4 1.4 copy.60
  263.8 0.7 copy.61
  264.5 0.1 add_select_fusion
  264.6 0.1 fusion.16
  264.7 0.1 maximum_select_fusion
  264.8 1.8 multiply_reduce_fusion
  266.8 0.5 copy-done.10
  267.3 0.1 dynamic_slice.6
  267.4 0.1 dynamic_slice.7
  267.4 0.1 copy-done.6
  267.5 0.1 reduce_sum.48
  267.7 0.1 pad_maximum_fusion.1
  267.7 0.1 multiply_multiply_fusion
  267.8 0.1 compare_convert_fusion
  267.9 0.6 dynamic-slice
  269.1 0.1 multiply_reduce_fusion.1
  269.2 91.2 %all-reduce.4.cloned.1.call-done = f32[16,3,2,32,32]{4,3,2,0,1:T(8,128)} async-done(((f32[16,3,2,32,32]{4,3,2,0,1:T(8,128)}), f32[16,3,2,32,32]{4,3,2,0,1:T(8,128)}) %all-reduce.4.cloned.1.call-update) | async-done | bytes 393232
  360.4 3.2 fusion
  363.6 3.2 fusion.1
  366.8 0.1 multiply_subtract_fusion
  366.9 0.7 convolution_subtract_fusion
  367.7 30.2 %all-reduce.1 = f32[3,2,64]{2,0,1:T(4,128)S(1)} all-reduce(f32[3,2,64]{2,0,1:T(4,128)S(1)} %copy.64), channel_id=3, replica_groups=mesh['cfg'=2,'tm'=16] {'tm'}, use_global_device_ids=true, to_apply=%region_6.7.clone | all-reduce | flops 384 | bytes 3072
  397.9 0.1 dynamic-slice_multiply_fusion
  398.0 0.6 copy.65
  (28 shorter events, 0.2 us)
Async XLA Ops:
  6.5 353.9 %all-reduce.4.cloned.1.call-start = ((), (), s32[]{:S(2)}) async-start(), calls=%async_computation | async-start | bytes 3145728
  19.7 3.2 copy-start
  42.4 3.4 copy-start.1
  45.8 2.8 copy-start.2
  213.1 4.5 %copy-start.3 = (bf16[6,32,2,64,256]{4,3,2,1,0:T(8,128)(2,1)}, bf16[6,32,2,64,256]{4,3,2,1,0:T(8,128)(2,1)S(1)}, u32[]{:S(2)}) copy-start(bf16[6,32,2,64,256]{4,3,2,1,0:T(8,128)(2,1)S(1)} %get-tuple-element.9.line) | copy-start | bytes 37748740
  217.7 3.5 copy-start.4
  263.8 0.9 copy-start.5
  264.8 1.9 copy-start.7
  266.6 0.7 copy-start.10
  266.6 0.7 copy-start.11
  266.6 0.9 copy-start.6
  266.6 1.2 copy-start.12
  360.4 6.5 %copy-start.8 = (s32[4096]{0:T(1024)S(1)}, s32[4096]{0:T(1024)}, u32[]{:S(2)}) copy-start(s32[4096]{0:T(1024)} %param.12) | copy-start | bytes 49156
  360.4 6.5 %copy-start.9 = (f32[4096]{0:T(1024)S(1)}, f32[4096]{0:T(1024)}, u32[]{:S(2)}) copy-start(f32[4096]{0:T(1024)} %param.11) | copy-start | bytes 49156
Sparse Core Ops, SparseCore 0:
  266.8 93.5 all-reduce.3

commit v2 on v1

--- a/solution.py
+++ b/solution.py
@@ -49,30 +49,6 @@
     return (far, far + 1, owner + 1 - 2 * (owner % 2))
 
 
-def pick_kernel(each, index, source, out):
-    owner = pl.program_id(0) // each
-    for place, quarter in enumerate(missing_quarters(owner)):
-        out[0, 0, place] = source[quarter, 0]
-
-
-def pick(quarters, index):
-    total = index.shape[0]
-    each = total // GROUP
-    _, _, _, rows, modes = quarters.shape
-    return pl.pallas_call(
-        functools.partial(pick_kernel, each),
-        grid_spec=pltpu.PrefetchScalarGridSpec(
-            num_scalar_prefetch=1,
-            grid=(total,),
-            in_specs=[pl.BlockSpec((GROUP, 1, 2, rows, modes), lambda e, index: (0, index[e], 0, 0, 0))],
-            out_specs=pl.BlockSpec(
-                (1, 1, 3, 2, rows, modes), lambda e, index: (e // each, e % each, 0, 0, 0, 0)
-            ),
-        ),
-        out_shape=jax.ShapeDtypeStruct((GROUP, each, 3, 2, rows, modes), jnp.bfloat16),
-    )(index, quarters)
-
-
 def other(rank, step):
     if step == 1:
         return rank + 1 - 2 * (rank % 2)
@@ -85,7 +61,9 @@
     return rank + side * (GROUP - 1 - 2 * rank)
 
 
-def exchange_kernel(n, lines, boxes, line_slots, box_slots, send_sem, recv_sem, local_sem):
+def exchange_kernel(
+    n, lines, index, line_slots, box_slots, boxes, send_sem, recv_sem, local_sem
+):
     me = lax.axis_index("tm")
     rank = me % GROUP
     base = me - rank
@@ -101,6 +79,14 @@
     for device in near + far:
         pl.semaphore_signal(barrier, inc=1, device_id={"tm": device}, device_id_type=MESH)
     pl.semaphore_wait(barrier, len(near) + len(far))
+
+    def choose(owner):
+        def body(entry, carry):
+            for place, quarter in enumerate(missing_quarters(owner)):
+                boxes[owner, entry, place] = lines[quarter, index[owner * 2 * half + entry]]
+            return carry
+
+        lax.fori_loop(0, 2 * half, body, 0)
 
     def copies(order, owner, device, slot, whole):
         box_from, box_to = boxes.at[owner], box_slots.at[slot]
@@ -122,14 +108,16 @@
 
     sent = []
     for order, peer in enumerate(peers):
-        sent += copies(order, peer, base + peer, slot_of(rank, peer // 2), True)
-        for copy in sent[-2:]:
-            copy.start()
+        sent.append(copies(order, peer, base + peer, slot_of(rank, peer // 2), True))
         if order < 2:
             owner = 2 * side + (rank + order) % 2
-            sent += copies(3 + order, owner, target + owner, GROUP + slot_of(rank, side), False)
-            for copy in sent[-2:]:
-                copy.start()
+            sent.append(copies(3 + order, owner, target + owner, GROUP + slot_of(rank, side), False))
+    for line_copy, _ in sent:
+        line_copy.start()
+    for owner in range(GROUP):
+        choose(owner)
+    for _, box_copy in sent:
+        box_copy.start()
     own = slot_of(rank, side)
     kept = [
         pltpu.make_async_copy(lines.at[rank], line_slots.at[own], local_sem.at[0]),
@@ -139,8 +127,9 @@
         copy.start()
     for copy in kept:
         copy.wait()
-    for copy in sent:
-        copy.wait_send()
+    for pair in sent:
+        for copy in pair:
+            copy.wait_send()
     for peer in peers:
         for copy in copies(0, rank, me, slot_of(peer, side), True):
             copy.wait_recv()
@@ -149,24 +138,141 @@
             copy.wait_recv()
 
 
-def exchange(n, lines, boxes):
+def exchange(n, lines, index):
+    _, inserts, _, rows, modes = lines.shape
+    each = index.shape[0] // GROUP
     return pl.pallas_call(
         functools.partial(exchange_kernel, n),
-        in_specs=[pl.BlockSpec(memory_space=pl.ANY)] * 2,
+        in_specs=[
+            pl.BlockSpec(memory_space=pltpu.VMEM),
+            pl.BlockSpec(memory_space=pltpu.SMEM),
+        ],
         out_specs=[pl.BlockSpec(memory_space=pl.ANY)] * 2,
         out_shape=[
-            jax.ShapeDtypeStruct((SLOTS, *lines.shape[1:]), jnp.bfloat16),
-            jax.ShapeDtypeStruct((SLOTS, *boxes.shape[1:]), jnp.bfloat16),
+            jax.ShapeDtypeStruct((SLOTS, inserts, 2, rows, modes), jnp.bfloat16),
+            jax.ShapeDtypeStruct((SLOTS, each, 3, 2, rows, modes), jnp.bfloat16),
         ],
         scratch_shapes=[
+            pltpu.VMEM((GROUP, each, 3, 2, rows, modes), jnp.bfloat16),
             pltpu.SemaphoreType.DMA((5, 2)),
             pltpu.SemaphoreType.DMA((SLOTS, 2)),
             pltpu.SemaphoreType.DMA((2,)),
         ],
         compiler_params=pltpu.CompilerParams(
-            collective_id=0, has_side_effects=True, vmem_limit_bytes=2**20
+            collective_id=0, has_side_effects=True, vmem_limit_bytes=20 * 2**20
         ),
-    )(lines, boxes)
+    )(lines, index)
+
+
+def gather_loops_kernel(n, parts, total, landed, send_sem, recv_sem):
+    me = lax.axis_index("tm")
+    rank = me % GROUP
+    base = me - rank
+    side = rank // 2
+    peers = [other(rank, step) for step in (2, 3, 1)]
+    before = (base + n - GROUP) % n
+    behind = (base + GROUP) % n
+
+    barrier = pltpu.get_barrier_semaphore()
+    near = [base + peer for peer in peers]
+    far = [group + 2 * side + core for group in (before, behind) for core in range(2)]
+    for device in near + far:
+        pl.semaphore_signal(barrier, inc=1, device_id={"tm": device}, device_id_type=MESH)
+    pl.semaphore_wait(barrier, len(near) + len(far))
+
+    def copy_to(order, block, device, slot):
+        return pltpu.make_async_remote_copy(
+            src_ref=parts.at[block],
+            dst_ref=landed.at[slot],
+            send_sem=send_sem.at[order],
+            recv_sem=recv_sem.at[slot],
+            device_id={"tm": device},
+            device_id_type=MESH,
+        )
+
+    sent = [copy_to(3 + core, core, before + 2 * side + core, GROUP + rank % 2) for core in range(2)]
+    sent += [copy_to(order, 2 + peer, base + peer, rank) for order, peer in enumerate(peers)]
+    for copy in sent:
+        copy.start()
+    for slot in peers + [GROUP, GROUP + 1]:
+        copy_to(0, 0, me, slot).wait_recv()
+    value = parts[2 + rank]
+    for slot in peers + [GROUP, GROUP + 1]:
+        value += landed[slot]
+    total[...] = value
+    for copy in sent:
+        copy.wait_send()
+
+
+def gather_loops(n, parts):
+    return pl.pallas_call(
+        functools.partial(gather_loops_kernel, n),
+        in_specs=[pl.BlockSpec(memory_space=pltpu.VMEM)],
+        out_specs=pl.BlockSpec(memory_space=pltpu.VMEM),
+        out_shape=jax.ShapeDtypeStruct(parts.shape[1:], jnp.float32),
+        scratch_shapes=[
+            pltpu.VMEM((SLOTS, *parts.shape[1:]), jnp.float32),
+            pltpu.SemaphoreType.DMA((5,)),
+            pltpu.SemaphoreType.DMA((SLOTS,)),
+        ],
+        compiler_params=pltpu.CompilerParams(collective_id=1, has_side_effects=True),
+    )(parts)
+
+
+def sum_all_kernel(n, part, total, landed, send_sem, recv_sem):
+    me = lax.axis_index("tm")
+    barrier = pltpu.get_barrier_semaphore()
+
+    def greet(step, carry):
+        pl.semaphore_signal(barrier, inc=1, device_id={"tm": (me + step) % n}, device_id_type=MESH)
+        return carry
+
+    lax.fori_loop(1, n, greet, 0)
+    pl.semaphore_wait(barrier, n - 1)
+
+    def copy_to(step, slot):
+        return pltpu.make_async_remote_copy(
+            src_ref=part,
+            dst_ref=landed.at[slot],
+            send_sem=send_sem.at[step],
+            recv_sem=recv_sem.at[slot],
+            device_id={"tm": (me + step) % n},
+            device_id_type=MESH,
+        )
+
+    def send(step, carry):
+        copy_to(step, me).start()
+        return carry
+
+    lax.fori_loop(1, n, send, 0)
+
+    def receive(step, value):
+        slot = (me + step) % n
+        copy_to(step, slot).wait_recv()
+        return value + landed[slot]
+
+    total[...] = lax.fori_loop(1, n, receive, part[...])
+
+    def finish(step, carry):
+        copy_to(step, me).wait_send()
+        return carry
+
+    lax.fori_loop(1, n, finish, 0)
+
+
+def sum_all(n, part):
+    return pl.pallas_call(
+        functools.partial(sum_all_kernel, n),
+        in_specs=[pl.BlockSpec(memory_space=pltpu.VMEM)],
+        out_specs=pl.BlockSpec(memory_space=pltpu.VMEM),
+        out_shape=jax.ShapeDtypeStruct(part.shape, jnp.float32),
+        scratch_shapes=[
+            pltpu.VMEM((n, *part.shape), jnp.float32),
+            pltpu.SemaphoreType.DMA((n,)),
+            pltpu.SemaphoreType.DMA((n,)),
+        ],
+        compiler_params=pltpu.CompilerParams(collective_id=2, has_side_effects=True),
+    )(part)
 
 
 def pairs_kernel(terms, index, where, line, box, gram, traces, flat, plain, turned):
@@ -286,8 +392,7 @@
     index = jnp.transpose(by_owner.reshape(GROUP, terms, 2, 2), (0, 3, 1, 2)).reshape(-1)
 
     lines = dress(meson_fields[:, :, 0], perambulators[:, 0], 4)
-    boxes = pick(lines, index)
-    line_slots, box_slots = exchange(n, lines, boxes)
+    line_slots, box_slots = exchange(n, lines, index)
     gram, traces = pairs(index, rank, line_slots, box_slots)
 
     gram = gram.reshape(GROUP, SEPARATIONS, inserts, 2, inserts, 2)
@@ -295,14 +400,16 @@
     loop_imag = gram[:, :, :, 1, :, 0] - gram[:, :, :, 0, :, 1]
     parts = jnp.stack([loop_real, loop_imag], 2)
     flipped = jnp.stack([jnp.swapaxes(loop_real, 2, 3), -jnp.swapaxes(loop_imag, 2, 3)], 2)
-    parts = jnp.where(right, flipped, parts)
-    slot = jnp.arange(GROUP, dtype=jnp.int32)[:, None]
-    apart = jnp.arange(SEPARATIONS, dtype=jnp.int32)[None]
-    sink_time = jnp.where(right, base + GROUP - 1 - slot - apart, base + slot) % n
-    hot = (sink_time[..., None] == jnp.arange(n, dtype=jnp.int32)).astype(jnp.float32)
-    spread = jnp.sum(hot[..., None, None, None] * parts[:, :, None], axis=0)
-    spread = jnp.transpose(spread, (1, 0, 2, 3, 4))
-    loops = lax.psum_scatter(spread, "tm", scatter_dimension=0, tiled=True)[0]
+    zero = jnp.zeros_like(parts[0, 0])
+    from_left, from_right = [], []
+    for v in range(SLOTS):
+        for k in range(SEPARATIONS):
+            slot = SLOTS - 1 - k - v
+            from_left.append(parts[v - 2, k] if v >= 2 else zero)
+            from_right.append(flipped[slot, k] if 0 <= slot < GROUP else zero)
+    blocks = jnp.where(right, jnp.stack(from_right), jnp.stack(from_left))
+    loops = gather_loops(n, blocks.reshape(SLOTS, -1, 128))
+    loops = loops.reshape(SEPARATIONS, 2, inserts, inserts)
 
     inserted = jnp.arange(inserts, dtype=jnp.int32)[:, None]
     hots = [(direct_ins[:, p][None] == inserted).astype(jnp.float32) for p in range(4)]
@@ -326,8 +433,12 @@
     weighted = traces * coef[None, :, None] * sign
     box_sum = jnp.sum(weighted[..., None] * box_hot[None, :, None], axis=1)
 
-    total = lax.psum_scatter(direct_sum - box_sum, "tm", scatter_dimension=2, tiled=True)
-    return total / n
+    partial = (direct_sum - box_sum).reshape(2 * SEPARATIONS, entries)
+    rows, lanes = -2 * SEPARATIONS % 8, -entries % 128
+    total = sum_all(n, jnp.pad(partial, ((0, rows), (0, lanes))))
+    share = entries // n
+    mine = lax.dynamic_slice(total, (0, me * share), (2 * SEPARATIONS, share))
+    return mine.reshape(SEPARATIONS, 2, share) / n
 
 
 ENTRY_DEV = 4

time: 407 us -> 258 us (0.63)
  waiting for transfers between devices: 91.2 us -> 0 us
  blocking collectives: 30.2 us -> 0 us
  between operations: 14.2 us -> 0.51 us
  Pallas kernels: 216 us -> 211 us
    unnamed x2 -> x0, waiting for transfers between devices: 91.2 us -> none
    unnamed x1 -> x0, blocking collectives: 30.2 us -> none
    pallas_call x1 -> x2, Pallas kernels: 19.5 us -> 13.4 us  [the longest x1 7.93 us: sum_all(): pl.pallas_call(functools.partial(sum_all_kernel, n), in_specs=[pl.BlockSp...]
    unnamed x27 -> x33, local copies, waits for them, and re-layouts: 18.6 us -> 15.6 us
  transfers between devices with their start and end apart: 1 -> 0, of which waited for: 1 -> 0; matrix products, arithmetic and copies ran while one was open for 0% -> 0% of each run, Pallas kernels for 0% -> 0%
where the time goes in v2:
time: 258 us
  Pallas kernels  211 us (82%)
  local copies, waits for them, and re-layouts  30.1 us (12%)
  other arithmetic  12.3 us (5%)
  matrix products  3.99 us (2%)
    pallas_call x1, Pallas kernels, exchange(): pl.pallas_call(functools.partial(exchange_kernel, n), in_specs=[pl.BlockS...  165 us
    pallas_call x1, Pallas kernels, pairs(): pl.pallas_call(functools.partial(pairs_kernel, terms), grid_spec=pltpu.Pr...  23.4 us
    unnamed x33, local copies, waits for them, and re-layouts  15.6 us
    neg x1, other arithmetic, local(): -jnp.swapaxes(loop_imag, 2, 3)  9.63 us
    pallas_call x1, Pallas kernels, dress(): pl.pallas_call(dress_kernel, grid=(inserts // block,), in_specs=[pl.Block...  9.01 us
    pallas_call x1, Pallas kernels, sum_all(): pl.pallas_call(functools.partial(sum_all_kernel, n), in_specs=[pl.BlockSp...  7.93 us
    pallas_call x1, Pallas kernels, gather_loops(): pl.pallas_call(functools.partial(gather_loops_kernel, n), in_specs=[pl.Bl...  5.47 us

profile of v2, /device:TPU:0, one launch (start us, length us, event | category | flops | bytes accessed | tf_op | source)
XLA Modules:
  0.0 257.8 jit_solution(7528454913137131987)
XLA Ops:
  0.0 1.0 slice_bitcast_fusion
  1.0 0.9 fusion.63
  2.0 0.1 pad_maximum_fusion.taus
  2.0 0.0 copy-start.9
  2.0 9.0 %shard_map.82.lines = bf16[4,32,2,64,256]{4,3,2,1,0:T(8,128)(2,1)S(1)} custom-call(bf16[2,32,256,256]{3,2,1,0:T(8,128)(2,1)} %bitcast.149, bf16[2,256,512]{2,1,0:T(8,128)(2,1)S(1)} %pad_maximum_fusion.taus), custom_call_target="tpu_custom_call" | custom-call | tf_op jit(solution)/shard_map/pallas_call | solution.py:34
  11.1 3.2 %copy-done = bf16[4,32,2,64,256]{4,3,2,1,0:T(8,128)(2,1)} copy-done((bf16[4,32,2,64,256]{4,3,2,1,0:T(8,128)(2,1)}, bf16[4,32,2,64,256]{4,3,2,1,0:T(8,128)(2,1)S(1)}, u32[]{:S(2)}) %copy-start) | copy-done | bytes 8388632
  14.3 0.1 fusion.66
  14.3 0.1 copy.89
  14.4 0.1 rev.3
  14.5 0.1 concatenate.15
  14.6 0.1 copy.88
  14.7 0.1 concatenate.14
  14.8 0.1 copy.90
  14.9 0.1 reshape.149.index
  15.1 3.4 %copy-done.1 = bf16[4,32,2,64,256]{4,3,2,1,0:T(8,128)(2,1)S(1)} copy-done((bf16[4,32,2,64,256]{4,3,2,1,0:T(8,128)(2,1)S(1)}, bf16[4,32,2,64,256]{4,3,2,1,0:T(8,128)(2,1)}, u32[]{:S(2)}) %copy-start.1) | copy-done | bytes 8388632
  18.4 165.2 %shard_map.83 = (bf16[6,32,2,64,256]{4,3,2,1,0:T(8,128)(2,1)S(1)}, bf16[6,8,3,2,64,256]{5,4,3,2,1,0:T(8,128)(2,1)S(1)}) custom-call(bf16[4,32,2,64,256]{4,3,2,1,0:T(8,128)(2,1)S(1)} %copy-done.1, s32[32]{0:T(128)S(1)} %reshape.149.index), custom_call_target="tpu_custom_call" | custom-call | tf_op jit(solution)/shard_map/pallas_call | solution.py:144
  183.6 4.5 %copy-done.2 = bf16[6,32,2,64,256]{4,3,2,1,0:T(8,128)(2,1)} copy-done((bf16[6,32,2,64,256]{4,3,2,1,0:T(8,128)(2,1)}, bf16[6,32,2,64,256]{4,3,2,1,0:T(8,128)(2,1)S(1)}, u32[]{:S(2)}) %copy-start.2) | copy-done | bytes 12582936
  188.2 3.5 %copy-done.3 = bf16[6,8,3,2,64,256]{5,4,3,2,1,0:T(8,128)(2,1)} copy-done((bf16[6,8,3,2,64,256]{5,4,3,2,1,0:T(8,128)(2,1)}, bf16[6,8,3,2,64,256]{5,4,3,2,1,0:T(8,128)(2,1)S(1)}, u32[]{:S(2)}) %copy-start.3) | copy-done | bytes 9437208
  191.7 23.4 %shard_map.84 = (f32[4,3,64,64]{3,2,1,0:T(8,128)}, f32[3,2,2,8,256]{4,3,2,1,0:T(8,128)}) custom-call(s32[32]{0:T(128)} %copy-done.4, s32[1]{0:T(128)} %bitcast.2.where, bf16[6,32,2,64,256]{4,3,2,1,0:T(8,128)(2,1)} %copy-done.2, bf16[6,8,3,2,64,256]{5,4,3,2,1,0:T(8,128)(2,1)} %copy-done.3), custom_call_target="tpu_custom_call" | custom-call | tf_op jit(solution)/shard_map/pallas_call | solution.py:344
  215.1 5.0 %copy.91 = f32[4,3,64,64]{0,3,2,1:T(8,128)} copy(f32[4,3,64,64]{3,2,1,0:T(8,128)} %get-tuple-element.11) | data formatting | bytes 393216 | tf_op jit(solution)/shard_map/pallas_call | solution.py:344
  220.1 9.6 %fusion.64 = (f32[4,3,32,1,32,1]{0,5,4,3,2,1:T(1,128)S(1)}, f32[4,3,32,1,32,1]{0,5,4,3,2,1:T(1,128)}, f32[4,3,32,1,32,1]{0,5,4,3,2,1:T(1,128)S(1)}) fusion(f32[4,3,32,2,32,2]{0,5,4,3,2,1:T(2,128)} %bitcast.146), kind=kLoop, calls=%fused_computation.162 | loop fusion | flops 36864 | bytes 344064 | tf_op jit(solution)/shard_map/neg | solution.py:402
  229.7 0.7 copy.94
  230.4 2.2 copy.95
  232.8 0.8 copy-done.5
  233.6 0.9 copy.92
  234.5 0.9 copy.93
  235.6 0.0 copy-start.8
  235.7 0.1 broadcast_select_fusion
  235.8 0.0 copy-start.12
  235.9 0.0 copy-start.13
  235.9 0.8 select_n.33.parts
  236.7 5.5 %shard_map.85 = f32[48,128]{1,0:T(8,128)} custom-call(f32[6,48,128]{2,1,0:T(8,128)} %select_n.33.parts), custom_call_target="tpu_custom_call" | custom-call | tf_op jit(solution)/shard_map/pallas_call | solution.py:208
  242.2 0.8 reshape.151
  243.1 1.6 fusion
  244.8 1.6 fusion.1
  246.5 0.1 multiply_subtract_fusion
  246.6 0.1 dynamic_slice.9
  246.7 0.1 reduce_sum.38
  246.8 0.1 pad_maximum_fusion.3
  246.9 0.1 multiply_multiply_fusion
  247.0 0.1 dynamic_slice.10
  247.0 0.1 compare_convert_fusion
  247.1 0.1 multiply_reduce_fusion
  247.2 0.7 convolution_subtract_fusion
  247.9 0.6 pad.4.part
  248.5 7.9 %shard_map.86 = f32[8,128]{1,0:T(8,128)} custom-call(f32[8,128]{1,0:T(8,128)} %pad.4.part), custom_call_target="tpu_custom_call" | custom-call | tf_op jit(solution)/shard_map/pallas_call | solution.py:264
  256.5 0.8 dynamic-slice_multiply_fusion
  257.2 0.6 div.6
  (55 shorter events, 0.4 us)
Async XLA Ops:
  2.0 12.3 %copy-start.9 = (s32[8,4]{0,1:T(4,128)S(1)}, s32[8,4]{0,1:T(4,128)}, u32[]{:S(2)}) copy-start(s32[8,4]{0,1:T(4,128)} %param.13) | copy-start | bytes 388
  11.0 3.2 %copy-start = (bf16[4,32,2,64,256]{4,3,2,1,0:T(8,128)(2,1)}, bf16[4,32,2,64,256]{4,3,2,1,0:T(8,128)(2,1)S(1)}, u32[]{:S(2)}) copy-start(bf16[4,32,2,64,256]{4,3,2,1,0:T(8,128)(2,1)S(1)} %shard_map.82.lines) | copy-start | bytes 25165828
  15.0 3.4 %copy-start.1 = (bf16[4,32,2,64,256]{4,3,2,1,0:T(8,128)(2,1)S(1)}, bf16[4,32,2,64,256]{4,3,2,1,0:T(8,128)(2,1)}, u32[]{:S(2)}) copy-start(bf16[4,32,2,64,256]{4,3,2,1,0:T(8,128)(2,1)} %copy-done) | copy-start | bytes 25165828
  18.4 165.2 %copy-start.4 = (s32[32]{0:T(128)}, s32[32]{0:T(128)S(1)}, u32[]{:S(2)}) copy-start(s32[32]{0:T(128)S(1)} %reshape.149.index) | copy-start | bytes 388
  183.6 4.5 %copy-start.2 = (bf16[6,32,2,64,256]{4,3,2,1,0:T(8,128)(2,1)}, bf16[6,32,2,64,256]{4,3,2,1,0:T(8,128)(2,1)S(1)}, u32[]{:S(2)}) copy-start(bf16[6,32,2,64,256]{4,3,2,1,0:T(8,128)(2,1)S(1)} %get-tuple-element.9.line) | copy-start | bytes 37748740
  188.1 3.5 %copy-start.3 = (bf16[6,8,3,2,64,256]{5,4,3,2,1,0:T(8,128)(2,1)}, bf16[6,8,3,2,64,256]{5,4,3,2,1,0:T(8,128)(2,1)S(1)}, u32[]{:S(2)}) copy-start(bf16[6,8,3,2,64,256]{5,4,3,2,1,0:T(8,128)(2,1)S(1)} %get-tuple-element.10.box) | copy-start | bytes 28311556
  232.8 0.8 copy-start.5
  234.5 1.2 copy-start.6
  235.6 7.5 %copy-start.8 = (s32[4096,4]{0,1:T(4,128)S(1)}, s32[4096,4]{0,1:T(4,128)}, u32[]{:S(2)}) copy-start(s32[4096,4]{0,1:T(4,128)} %param.10) | copy-start | bytes 196612
  235.8 10.8 %copy-start.12 = (f32[8]{0:T(128)S(1)}, f32[8]{0:T(128)}, u32[]{:S(2)}) copy-start(f32[8]{0:T(128)} %param.14) | copy-start | bytes 100
  235.9 10.8 %copy-start.7 = (f32[3,2,2,8,256]{4,3,2,1,0:T(8,128)S(1)}, f32[3,2,2,8,256]{4,3,2,1,0:T(8,128)}, u32[]{:S(2)}) copy-start(f32[3,2,2,8,256]{4,3,2,1,0:T(8,128)} %get-tuple-element.12) | copy-start | bytes 294916
  235.9 11.1 %copy-start.13 = (s32[8]{0:T(128)S(1)}, s32[8]{0:T(128)}, u32[]{:S(2)}) copy-start(s32[8]{0:T(128)} %param.15) | copy-start | bytes 100
  235.9 11.3 %copy-start.10 = (s32[4096]{0:T(1024)S(1)}, s32[4096]{0:T(1024)}, u32[]{:S(2)}) copy-start(s32[4096]{0:T(1024)} %param.12) | copy-start | bytes 49156
  235.9 11.3 %copy-start.11 = (f32[4096]{0:T(1024)S(1)}, f32[4096]{0:T(1024)}, u32[]{:S(2)}) copy-start(f32[4096]{0:T(1024)} %param.11) | copy-start | bytes 49156

commit v3 on v2

--- a/solution.py
+++ b/solution.py
@@ -23,7 +23,7 @@
     both = both.astype(jnp.bfloat16).reshape(count, GROUP, rows // GROUP, 2 * rows)
     for quarter in range(GROUP):
         for part in range(2):
-            out[quarter, :, part] = both[:, quarter, :, part * rows : (part + 1) * rows]
+            out[quarter, part] = both[:, quarter, :, part * rows : (part + 1) * rows]
 
 
 def dress(fields, perambulators, block):
@@ -38,8 +38,8 @@
             pl.BlockSpec((2, block, modes, modes), lambda g: (0, g, 0, 0)),
             pl.BlockSpec((2, modes, 2 * modes), lambda g: (0, 0, 0)),
         ],
-        out_specs=pl.BlockSpec((GROUP, block, 2, modes // GROUP, modes), lambda g: (0, g, 0, 0, 0)),
-        out_shape=jax.ShapeDtypeStruct((GROUP, inserts, 2, modes // GROUP, modes), jnp.bfloat16),
+        out_specs=pl.BlockSpec((GROUP, 2, block, modes // GROUP, modes), lambda g: (0, 0, g, 0, 0)),
+        out_shape=jax.ShapeDtypeStruct((GROUP, 2, inserts, modes // GROUP, modes), jnp.bfloat16),
         compiler_params=pltpu.CompilerParams(vmem_limit_bytes=40 * 2**20),
     )(fields, taus)
 
@@ -62,7 +62,7 @@
 
 
 def exchange_kernel(
-    n, lines, index, line_slots, box_slots, boxes, send_sem, recv_sem, local_sem
+    n, lines, index, line_slots, box_slots, held, boxes, send_sem, recv_sem, local_sem
 ):
     me = lax.axis_index("tm")
     rank = me % GROUP
@@ -82,8 +82,10 @@
 
     def choose(owner):
         def body(entry, carry):
+            ins = index[owner * 2 * half + entry]
             for place, quarter in enumerate(missing_quarters(owner)):
-                boxes[owner, entry, place] = lines[quarter, index[owner * 2 * half + entry]]
+                for part in range(2):
+                    boxes[owner, entry, place, part] = held[quarter, part, ins]
             return carry
 
         lax.fori_loop(0, 2 * half, body, 0)
@@ -112,8 +114,11 @@
         if order < 2:
             owner = 2 * side + (rank + order) % 2
             sent.append(copies(3 + order, owner, target + owner, GROUP + slot_of(rank, side), False))
+    keep = pltpu.make_async_copy(lines, held, local_sem.at[2])
+    keep.start()
     for line_copy, _ in sent:
         line_copy.start()
+    keep.wait()
     for owner in range(GROUP):
         choose(owner)
     for _, box_copy in sent:
@@ -139,24 +144,25 @@
 
 
 def exchange(n, lines, index):
-    _, inserts, _, rows, modes = lines.shape
+    _, _, inserts, rows, modes = lines.shape
     each = index.shape[0] // GROUP
     return pl.pallas_call(
         functools.partial(exchange_kernel, n),
         in_specs=[
-            pl.BlockSpec(memory_space=pltpu.VMEM),
+            pl.BlockSpec(memory_space=pl.ANY),
             pl.BlockSpec(memory_space=pltpu.SMEM),
         ],
         out_specs=[pl.BlockSpec(memory_space=pl.ANY)] * 2,
         out_shape=[
-            jax.ShapeDtypeStruct((SLOTS, inserts, 2, rows, modes), jnp.bfloat16),
+            jax.ShapeDtypeStruct((SLOTS, 2, inserts, rows, modes), jnp.bfloat16),
             jax.ShapeDtypeStruct((SLOTS, each, 3, 2, rows, modes), jnp.bfloat16),
         ],
         scratch_shapes=[
+            pltpu.VMEM(lines.shape, jnp.bfloat16),
             pltpu.VMEM((GROUP, each, 3, 2, rows, modes), jnp.bfloat16),
             pltpu.SemaphoreType.DMA((5, 2)),
             pltpu.SemaphoreType.DMA((SLOTS, 2)),
-            pltpu.SemaphoreType.DMA((2,)),
+            pltpu.SemaphoreType.DMA((3,)),
         ],
         compiler_params=pltpu.CompilerParams(
             collective_id=0, has_side_effects=True, vmem_limit_bytes=20 * 2**20
@@ -275,9 +281,9 @@
     )(part)
 
 
-def pairs_kernel(terms, index, where, line, box, gram, traces, flat, plain, turned):
+def pairs_kernel(terms, index, where, line, box, loops, traces, flat, plain, turned):
     slot = pl.program_id(0)
-    inserts, _, rows, modes = line.shape[1:]
+    _, inserts, rows, modes = line.shape[1:]
     owner = where[0]
     side = owner // 2
     each = 4 * terms
@@ -285,6 +291,7 @@
     @pl.when(slot == 0)
     def _():
         traces[...] = jnp.zeros_like(traces)
+        loops[...] = jnp.zeros_like(loops)
 
     step = 16
     for start in range(0, rows, step):
@@ -311,7 +318,7 @@
         for place, quarter in enumerate(quarters):
             fill(quarter, (box[0, entry, place, 0], box[0, entry, place, 1]))
         ins = index[owner * each + entry]
-        fill(owner, (line[0, ins, 0], line[0, ins, 1]))
+        fill(owner, (line[0, 0, ins], line[0, 1, ins]))
 
     contract = (((1,), (1,)), ((), ()))
     for k in range(SEPARATIONS):
@@ -319,9 +326,15 @@
 
         @pl.when((sink >= 0) & (sink < GROUP))
         def _(k=k, sink=sink):
-            gram[sink, k] = lax.dot_general(
-                flat[sink], flat[slot], contract, preferred_element_type=jnp.float32
+            gram = lax.dot_general(
+                flat[sink + side * k],
+                flat[slot - side * k],
+                contract,
+                preferred_element_type=jnp.float32,
             )
+            block = jnp.where(side == 0, sink + 2, SLOTS - 1 - k - sink)
+            loops[block, k, 0] = gram[:inserts, :inserts] + gram[inserts:, inserts:]
+            loops[block, k, 1] = gram[inserts:, :inserts] - gram[:inserts, inserts:]
             for term in range(terms):
                 a, a_turned = plain[sink, 2 * term], turned[sink, term]
                 c = plain[sink, 2 * term + 1]
@@ -338,7 +351,7 @@
 
 
 def pairs(index, rank, line_slots, box_slots):
-    _, inserts, _, rows, modes = line_slots.shape
+    _, _, inserts, rows, modes = line_slots.shape
     each = box_slots.shape[1]
     terms = each // 4
     return pl.pallas_call(
@@ -347,11 +360,11 @@
             num_scalar_prefetch=2,
             grid=(SLOTS,),
             in_specs=[
-                pl.BlockSpec((1, inserts, 2, rows, modes), lambda s, *_: (s, 0, 0, 0, 0)),
+                pl.BlockSpec((1, 2, inserts, rows, modes), lambda s, *_: (s, 0, 0, 0, 0)),
                 pl.BlockSpec((1, each, 3, 2, rows, modes), lambda s, *_: (s, 0, 0, 0, 0, 0)),
             ],
             out_specs=[
-                pl.BlockSpec((GROUP, SEPARATIONS, 2 * inserts, 2 * inserts), lambda s, *_: (0, 0, 0, 0)),
+                pl.BlockSpec((SLOTS, SEPARATIONS, 2, inserts, inserts), lambda s, *_: (0, 0, 0, 0, 0)),
                 pl.BlockSpec((SEPARATIONS, terms, 2, 8, modes), lambda s, *_: (0, 0, 0, 0, 0)),
             ],
             scratch_shapes=[
@@ -361,7 +374,7 @@
             ],
         ),
         out_shape=[
-            jax.ShapeDtypeStruct((GROUP, SEPARATIONS, 2 * inserts, 2 * inserts), jnp.float32),
+            jax.ShapeDtypeStruct((SLOTS, SEPARATIONS, 2, inserts, inserts), jnp.float32),
             jax.ShapeDtypeStruct((SEPARATIONS, terms, 2, 8, modes), jnp.float32),
         ],
         compiler_params=pltpu.CompilerParams(vmem_limit_bytes=56 * 2**20),
@@ -382,7 +395,6 @@
     n = lax.axis_size("tm")
     me = lax.axis_index("tm")
     rank = me % GROUP
-    base = me - rank
     right = rank >= 2
     inserts = meson_fields.shape[1]
     terms = box_ins.shape[0] // GROUP
@@ -393,23 +405,8 @@
 
     lines = dress(meson_fields[:, :, 0], perambulators[:, 0], 4)
     line_slots, box_slots = exchange(n, lines, index)
-    gram, traces = pairs(index, rank, line_slots, box_slots)
-
-    gram = gram.reshape(GROUP, SEPARATIONS, inserts, 2, inserts, 2)
-    loop_real = gram[:, :, :, 0, :, 0] + gram[:, :, :, 1, :, 1]
-    loop_imag = gram[:, :, :, 1, :, 0] - gram[:, :, :, 0, :, 1]
-    parts = jnp.stack([loop_real, loop_imag], 2)
-    flipped = jnp.stack([jnp.swapaxes(loop_real, 2, 3), -jnp.swapaxes(loop_imag, 2, 3)], 2)
-    zero = jnp.zeros_like(parts[0, 0])
-    from_left, from_right = [], []
-    for v in range(SLOTS):
-        for k in range(SEPARATIONS):
-            slot = SLOTS - 1 - k - v
-            from_left.append(parts[v - 2, k] if v >= 2 else zero)
-            from_right.append(flipped[slot, k] if 0 <= slot < GROUP else zero)
-    blocks = jnp.where(right, jnp.stack(from_right), jnp.stack(from_left))
-    loops = gather_loops(n, blocks.reshape(SLOTS, -1, 128))
-    loops = loops.reshape(SEPARATIONS, 2, inserts, inserts)
+    blocks, traces = pairs(index, rank, line_slots, box_slots)
+    loops = gather_loops(n, blocks)
 
     inserted = jnp.arange(inserts, dtype=jnp.int32)[:, None]
     hots = [(direct_ins[:, p][None] == inserted).astype(jnp.float32) for p in range(4)]

time: 258 us -> 242 us (0.938)
  local copies, waits for them, and re-layouts: 30.1 us -> 17.9 us
  other arithmetic: 12.3 us -> 2.39 us
  Pallas kernels: 211 us -> 215 us
    neg x1 -> x0, other arithmetic: 9.63 us -> none  [local(): -jnp.swapaxes(loop_imag, 2, 3)]
    pallas_call x1 -> x0, local copies, waits for them, and re-layouts: 5 us -> none  [pairs(): pl.pallas_call(functools.partial(pairs_kernel, terms), grid_spec=pltpu.Pr...]
    pallas_call x1, Pallas kernels: 5.47 us -> 8.67 us  [gather_loops(): pl.pallas_call(functools.partial(gather_loops_kernel, n), in_specs=[pl.Bl...]
    unnamed x33 -> x24, local copies, waits for them, and re-layouts: 15.6 us -> 14.7 us
where the time goes in v3:
time: 242 us; the launch traced here: 241 us
  Pallas kernels  215 us (89%)
  local copies, waits for them, and re-layouts  17.9 us (7%)
  matrix products  5.77 us (2%)
    pallas_call x1, Pallas kernels, exchange(): pl.pallas_call(functools.partial(exchange_kernel, n), in_specs=[pl.BlockS...  166 us
    pallas_call x1, Pallas kernels, pairs(): pl.pallas_call(functools.partial(pairs_kernel, terms), grid_spec=pltpu.Pr...  23.8 us
    unnamed x24, local copies, waits for them, and re-layouts  14.7 us
    pallas_call x1, Pallas kernels, dress(): pl.pallas_call(dress_kernel, grid=(inserts // block,), in_specs=[pl.Block...  9 us
    pallas_call x1, Pallas kernels, gather_loops(): pl.pallas_call(functools.partial(gather_loops_kernel, n), in_specs=[pl.Bl...  8.67 us
    pallas_call x1, Pallas kernels, sum_all(): pl.pallas_call(functools.partial(sum_all_kernel, n), in_specs=[pl.BlockSp...  7.93 us
    dot_general x2, matrix products, lookup(): picked = jnp.einsum('kcab,al->kcbl', loops, row_hot, precision=HIGHEST)  5.04 us

profile of v3, /device:TPU:0, one launch (start us, length us, event | category | flops | bytes accessed | tf_op | source)
XLA Modules:
  0.0 241.4 jit_solution(1241441279067494082)
XLA Ops:
  0.0 1.0 slice_bitcast_fusion
  1.0 0.9 fusion.17
  2.0 0.1 pad_maximum_fusion.taus
  2.0 0.0 copy-start.7
  2.0 9.0 %shard_map.82.lines = bf16[4,2,32,64,256]{4,3,2,1,0:T(8,128)(2,1)S(1)} custom-call(bf16[2,32,256,256]{3,2,1,0:T(8,128)(2,1)} %bitcast.35, bf16[2,256,512]{2,1,0:T(8,128)(2,1)S(1)} %pad_maximum_fusion.taus), custom_call_target="tpu_custom_call" | custom-call | tf_op jit(solution)/shard_map/pallas_call | solution.py:34
  11.0 0.0 copy-start
  11.0 3.2 %copy-done = bf16[4,2,32,64,256]{4,3,2,1,0:T(8,128)(2,1)} copy-done((bf16[4,2,32,64,256]{4,3,2,1,0:T(8,128)(2,1)}, bf16[4,2,32,64,256]{4,3,2,1,0:T(8,128)(2,1)S(1)}, u32[]{:S(2)}) %copy-start) | copy-done | bytes 8388632
  14.3 0.0 copy-done.7
  14.3 0.1 fusion.19
  14.3 0.1 copy.29
  14.4 0.1 rev.3
  14.5 0.1 concatenate.15
  14.6 0.1 copy.28
  14.7 0.1 concatenate.14
  14.8 0.1 copy.30
  15.0 0.1 reshape.99.index
  15.0 0.0 copy-start.1
  15.1 3.4 %copy-done.1 = bf16[4,2,32,64,256]{4,3,2,1,0:T(8,128)(2,1)S(1)} copy-done((bf16[4,2,32,64,256]{4,3,2,1,0:T(8,128)(2,1)S(1)}, bf16[4,2,32,64,256]{4,3,2,1,0:T(8,128)(2,1)}, u32[]{:S(2)}) %copy-start.1) | copy-done | bytes 8388632
  18.4 165.7 %shard_map.83 = (bf16[6,2,32,64,256]{4,3,2,1,0:T(8,128)(2,1)S(1)}, bf16[6,8,3,2,64,256]{5,4,3,2,1,0:T(8,128)(2,1)S(1)}) custom-call(bf16[4,2,32,64,256]{4,3,2,1,0:T(8,128)(2,1)S(1)} %copy-done.1, s32[32]{0:T(128)S(1)} %reshape.99.index), custom_call_target="tpu_custom_call" | custom-call | tf_op jit(solution)/shard_map/pallas_call | solution.py:149
  184.2 0.0 copy-done.4
  184.2 0.0 copy-start.2
  184.2 4.5 %copy-done.2 = bf16[6,2,32,64,256]{4,3,2,1,0:T(8,128)(2,1)} copy-done((bf16[6,2,32,64,256]{4,3,2,1,0:T(8,128)(2,1)}, bf16[6,2,32,64,256]{4,3,2,1,0:T(8,128)(2,1)S(1)}, u32[]{:S(2)}) %copy-start.2) | copy-done | bytes 12582936
  188.7 3.6 %copy-done.3 = bf16[6,8,3,2,64,256]{5,4,3,2,1,0:T(8,128)(2,1)} copy-done((bf16[6,8,3,2,64,256]{5,4,3,2,1,0:T(8,128)(2,1)}, bf16[6,8,3,2,64,256]{5,4,3,2,1,0:T(8,128)(2,1)S(1)}, u32[]{:S(2)}) %copy-start.3) | copy-done | bytes 9437208
  192.3 23.8 %shard_map.84 = (f32[6,3,2,32,32]{4,3,2,1,0:T(8,128)}, f32[3,2,2,8,256]{4,3,2,1,0:T(8,128)}) custom-call(s32[32]{0:T(128)} %copy-done.4, s32[1]{0:T(128)} %bitcast.2.where, bf16[6,2,32,64,256]{4,3,2,1,0:T(8,128)(2,1)} %copy-done.2, bf16[6,8,3,2,64,256]{5,4,3,2,1,0:T(8,128)(2,1)} %copy-done.3), custom_call_target="tpu_custom_call" | custom-call | tf_op jit(solution)/shard_map/pallas_call | solution.py:357
  216.1 0.0 copy-start.8
  216.1 0.0 copy-start.9
  216.1 8.7 %shard_map.85 = f32[3,2,32,32]{3,2,1,0:T(8,128)} custom-call(f32[6,3,2,32,32]{4,3,2,1,0:T(8,128)} %get-tuple-element.11.parts), custom_call_target="tpu_custom_call" | custom-call | tf_op jit(solution)/shard_map/pallas_call | solution.py:214
  224.8 0.0 copy-done.6
  224.9 2.5 %fusion = f32[3,2,4096]{2,1,0:T(2,128)S(1)} fusion(f32[32,4096]{1,0:T(8,128)S(1)} %fusion.7, f32[3,2,32,32]{3,2,1,0:T(8,128)} %shard_map.85, s32[4096]{0:T(1024)S(1)} %bitcast.39), kind=kOutput, calls=%fused_computation.2 | convolution fusion | flops 303669248 | bytes 663552 | tf_op jit(solution)/shard_map/kcab,al->kcbl/dot_general | solution.py:415
  227.5 2.5 %fusion.1 = f32[3,2,4096]{2,1,0:T(2,128)S(1)} fusion(f32[32,4096]{1,0:T(8,128)S(1)} %fusion.10, f32[3,2,32,32]{3,2,1,0:T(8,128)} %shard_map.85, s32[4096]{0:T(1024)S(1)} %bitcast.38), kind=kOutput, calls=%fused_computation.3 | convolution fusion | flops 303669248 | bytes 663552 | tf_op jit(solution)/shard_map/kcab,al->kcbl/dot_general | solution.py:415
  230.0 0.1 multiply_subtract_fusion
  230.1 0.0 copy-done.5
  230.2 0.1 reduce_sum.38
  230.3 0.0 copy-done.10
  230.3 0.1 dynamic_slice.9
  230.4 0.1 pad_maximum_fusion.1
  230.4 0.1 multiply_multiply_fusion
  230.5 0.0 copy-done.11
  230.5 0.1 dynamic_slice.10
  230.6 0.1 compare_convert_fusion
  230.7 0.1 multiply_reduce_fusion
  230.7 0.0 copy-done.8
  230.7 0.0 copy-done.9
  230.8 0.7 convolution_subtract_fusion
  231.5 0.6 pad.4.part
  232.1 7.9 %shard_map.86 = f32[8,128]{1,0:T(8,128)} custom-call(f32[8,128]{1,0:T(8,128)} %pad.4.part), custom_call_target="tpu_custom_call" | custom-call | tf_op jit(solution)/shard_map/pallas_call | solution.py:270
  240.0 0.8 dynamic-slice_multiply_fusion
  240.8 0.6 div.6
  (12 shorter events, 0.2 us)
Async XLA Ops:
  2.0 12.3 %copy-start.7 = (s32[8,4]{0,1:T(4,128)S(1)}, s32[8,4]{0,1:T(4,128)}, u32[]{:S(2)}) copy-start(s32[8,4]{0,1:T(4,128)} %param.13) | copy-start | bytes 388
  11.0 3.2 %copy-start = (bf16[4,2,32,64,256]{4,3,2,1,0:T(8,128)(2,1)}, bf16[4,2,32,64,256]{4,3,2,1,0:T(8,128)(2,1)S(1)}, u32[]{:S(2)}) copy-start(bf16[4,2,32,64,256]{4,3,2,1,0:T(8,128)(2,1)S(1)} %shard_map.82.lines) | copy-start | bytes 25165828
  15.0 3.4 %copy-start.1 = (bf16[4,2,32,64,256]{4,3,2,1,0:T(8,128)(2,1)S(1)}, bf16[4,2,32,64,256]{4,3,2,1,0:T(8,128)(2,1)}, u32[]{:S(2)}) copy-start(bf16[4,2,32,64,256]{4,3,2,1,0:T(8,128)(2,1)} %copy-done) | copy-start | bytes 25165828
  18.4 165.8 %copy-start.4 = (s32[32]{0:T(128)}, s32[32]{0:T(128)S(1)}, u32[]{:S(2)}) copy-start(s32[32]{0:T(128)S(1)} %reshape.99.index) | copy-start | bytes 388
  184.2 4.5 %copy-start.2 = (bf16[6,2,32,64,256]{4,3,2,1,0:T(8,128)(2,1)}, bf16[6,2,32,64,256]{4,3,2,1,0:T(8,128)(2,1)S(1)}, u32[]{:S(2)}) copy-start(bf16[6,2,32,64,256]{4,3,2,1,0:T(8,128)(2,1)S(1)} %get-tuple-element.9.line) | copy-start | bytes 37748740
  188.7 3.6 %copy-start.3 = (bf16[6,8,3,2,64,256]{5,4,3,2,1,0:T(8,128)(2,1)}, bf16[6,8,3,2,64,256]{5,4,3,2,1,0:T(8,128)(2,1)S(1)}, u32[]{:S(2)}) copy-start(bf16[6,8,3,2,64,256]{5,4,3,2,1,0:T(8,128)(2,1)S(1)} %get-tuple-element.10.box) | copy-start | bytes 28311556
  192.3 32.5 %copy-start.6 = (s32[4096,4]{0,1:T(4,128)S(1)}, s32[4096,4]{0,1:T(4,128)}, u32[]{:S(2)}) copy-start(s32[4096,4]{0,1:T(4,128)} %param.10) | copy-start | bytes 196612
  216.1 14.1 %copy-start.5 = (f32[3,2,2,8,256]{4,3,2,1,0:T(8,128)S(1)}, f32[3,2,2,8,256]{4,3,2,1,0:T(8,128)}, u32[]{:S(2)}) copy-start(f32[3,2,2,8,256]{4,3,2,1,0:T(8,128)} %get-tuple-element.12) | copy-start | bytes 294916
  216.1 14.2 %copy-start.10 = (f32[8]{0:T(128)S(1)}, f32[8]{0:T(128)}, u32[]{:S(2)}) copy-start(f32[8]{0:T(128)} %param.14) | copy-start | bytes 100
  216.1 14.4 %copy-start.11 = (s32[8]{0:T(128)S(1)}, s32[8]{0:T(128)}, u32[]{:S(2)}) copy-start(s32[8]{0:T(128)} %param.15) | copy-start | bytes 100
  216.1 14.7 %copy-start.8 = (s32[4096]{0:T(1024)S(1)}, s32[4096]{0:T(1024)}, u32[]{:S(2)}) copy-start(s32[4096]{0:T(1024)} %param.12) | copy-start | bytes 49156
  216.1 14.6 %copy-start.9 = (f32[4096]{0:T(1024)S(1)}, f32[4096]{0:T(1024)}, u32[]{:S(2)}) copy-start(f32[4096]{0:T(1024)} %param.11) | copy-start | bytes 49156
